TPU v7x, 128 devices: a whole 4x4x4 slice. The times are simulated.
128 devices in a mesh: pix: 32 (over x, z, core), tp: 4 (over y).
Axes of the slice: x: 4, y: 4, z: 4, core: 2. Of those that a mesh axis runs over, the one named last changes fastest.
Arguments:
- latent: bfloat16 [131072, 512], P(('pix', 'tp')), may hold values from -6 to 6
- norm_gain: float32 [512], replicated, may hold values from 0.5 to 2
- w_in: bfloat16 [512, 2048], P(None, 'tp'), may hold values from -0.25 to 0.25
- w_out: bfloat16 [2048, 512], P('tp'), may hold values from -0.125 to 0.125
- send_rows: int32 [16384, 32], P(('pix', 'tp')), may hold values from 0 to 1023
- obs_src: int32 [524288], P(('pix', 'tp')), may hold values from 0 to 5119
- obs_feat: bfloat16 [524288, 128], P(('pix', 'tp')), may hold values from -6 to 6
- obs_inst: int32 [524288], P(('pix', 'tp')), may hold values from 0 to 31
- inst_embed: float32 [32, 2048], replicated, may hold values from -3 to 3
- w_dec: bfloat16 [512, 2048], replicated, may hold values from -0.25 to 0.25
- w_feat: bfloat16 [128, 2048], replicated, may hold values from -0.5 to 0.5
- w_head: bfloat16 [2048, 128], replicated, may hold values from -0.125 to 0.125
Outputs:
- latent_out: bfloat16 [131072, 512], P(('pix', 'tp'))
- decoded: float32 [524288, 128], P(('pix', 'tp'))
All inputs are finite; a program needn't handle non-finite values.
Results may differ from a plain program's by a relative error of at most 0.005.
Values may be sent and summed in bfloat16 or wider, within the bound.
A program may use at most 64 MiB of HBM per device.

v0:
```python
import jax
import jax.numpy as jnp
from jax import lax
from jax.sharding import PartitionSpec as P


def layer_norm(block, norm_gain):
    values = block.astype(jnp.float32)
    center = values - jnp.mean(values, axis=-1, keepdims=True)
    spread = jnp.mean(center * center, axis=-1, keepdims=True)
    return (center * lax.rsqrt(spread + 1e-05) * norm_gain).astype(jnp.bfloat16)


def local(
    latent,
    norm_gain,
    w_in,
    w_out,
    send_rows,
    obs_src,
    obs_feat,
    obs_inst,
    inst_embed,
    w_dec,
    w_feat,
    w_head,
):
    normed = layer_norm(latent, norm_gain)
    inner = jax.nn.gelu(
        jnp.dot(
            lax.all_gather(normed, "tp", axis=0, tiled=True),
            w_in,
            preferred_element_type=jnp.float32,
        )
    ).astype(jnp.bfloat16)
    partials = jnp.dot(inner, w_out, preferred_element_type=jnp.float32)
    update = lax.psum_scatter(partials, "tp", scatter_dimension=0, tiled=True)
    updated = (latent.astype(jnp.float32) + update).astype(jnp.bfloat16)
    outgoing = jnp.take(updated, send_rows.reshape(-1), axis=0)
    arrived = lax.all_to_all(outgoing, ("pix", "tp"), split_axis=0, concat_axis=0, tiled=True)
    table = jnp.concatenate([updated, arrived], axis=0)
    count = obs_src.shape[0]
    block_rows = min(1024, count)
    nblocks = count // block_rows
    instruments = inst_embed.shape[0]

    def decode_block(items):
        sources, feats, insts = items
        gathered = jnp.take(table, sources, axis=0)
        pre = jnp.dot(gathered, w_dec, preferred_element_type=jnp.float32)
        pre = pre + jnp.dot(feats, w_feat, preferred_element_type=jnp.float32)
        one_hot = (insts[:, None] == jnp.arange(instruments, dtype=jnp.int32)[None, :]).astype(
            jnp.float32
        )
        pre = pre + jnp.dot(one_hot, inst_embed, precision=lax.Precision.HIGHEST)
        hidden = jax.nn.gelu(pre).astype(jnp.bfloat16)
        return jnp.dot(hidden, w_head, preferred_element_type=jnp.float32)

    decoded = lax.map(
        decode_block,
        (
            obs_src.reshape(nblocks, block_rows),
            obs_feat.reshape(nblocks, block_rows, obs_feat.shape[1]),
            obs_inst.reshape(nblocks, block_rows),
        ),
    )
    return (updated, decoded.reshape(count, w_head.shape[1]))


def solution(mesh):
    in_specs = (
        P(("pix", "tp"), None),
        P(),
        P(None, "tp"),
        P("tp", None),
        P(("pix", "tp"), None),
        P(("pix", "tp")),
        P(("pix", "tp"), None),
        P(("pix", "tp")),
        P(),
        P(),
        P(),
        P(),
    )
    out_specs = (P(("pix", "tp"), None), P(("pix", "tp"), None))
    return jax.shard_map(local, mesh=mesh, in_specs=in_specs, out_specs=out_specs, check_vma=False)
```

profile of v0, /device:TPU:27, one launch (start us, length us, event | category | flops | bytes accessed | tf_op | source)
XLA Modules:
  0.0 339.2 jit_solution(11346092847165351543)
XLA Ops:
  7.2 0.0 copy-start
  7.2 0.0 copy-start.7
  7.2 0.0 all-gather.2.cloned.1.call-start
  7.2 1.5 convert_reduce_fusion
  8.8 1.7 fusion.31
  10.5 2.6 fusion.33
  13.1 0.0 all-gather.2.cloned.1.call-update
  13.1 0.0 reduce-scatter.2.cloned.1.call-start
  13.2 48.8 %all-gather.2.cloned.1.call-done = bf16[4096,512]{1,0:T(8,128)(2,1)} async-done(((bf16[1024,512]{1,0:T(8,128)(2,1)}), bf16[4096,512]{1,0:T(8,128)(2,1)}) %all-gather.2.cloned.1.call-update) | async-done | bytes 4194320 | tf_op jit(solution)/shard_map/all_gather | solution.py:31
  62.0 0.0 copy-done
  62.0 0.0 copy-done.7
  62.0 9.2 %fusion.27 = f32[4096,512]{1,0:T(8,128)} fusion(bf16[512,512]{1,0:T(8,128)(2,1)S(1)} %copy-done, bf16[4096,512]{1,0:T(8,128)(2,1)} %all-gather.2.cloned.1.call-done, bf16[512,512]{1,0:T(8,128)(2,1)S(1)} %copy-done.7), kind=kOutput, calls=%fused_computation.40 | convolution fusion | flops 4313841664 | bytes 13631488 | tf_op jit(solution)/shard_map/dot_general | solution.py:36
  71.2 0.0 copy-start.4
  71.2 0.0 copy-start.2
  71.2 0.0 reduce-scatter.2.cloned.1.call-update
  71.2 0.7 copy-done.4
  71.9 0.1 copy.16
  72.0 0.1 reshape.110
  72.2 0.1 copy.15
  72.3 79.7 %reduce-scatter.2.cloned.1.call-done = f32[1024,512]{1,0:T(8,128)} async-done(((f32[4096,512]{1,0:T(8,128)}), f32[1024,512]{1,0:T(8,128)}) %reduce-scatter.2.cloned.1.call-update) | async-done | bytes 2097168 | tf_op jit(solution)/shard_map/reduce_scatter | solution.py:37
  152.1 0.0 copy-done.2
  152.1 1.9 fusion.34
  154.0 0.0 copy-start.1
  154.0 17.3 %gather_fusion.1 = bf16[4096,512]{1,0:T(8,128)(2,1)} fusion(bf16[1024,512]{1,0:T(8,128)(2,1)S(1)} %fusion.34, s32[4096]{0:T(1024)S(1)} %broadcast_clamp_fusion.1), kind=kCustom, calls=%fused_computation.1 | custom fusion | bytes 8404992 | tf_op jit(solution)/shard_map/jit(_take)/gather | solution.py:39
  171.3 3.9 %broadcast_select_fusion = bf16[128,32,512]{2,1,0:T(8,128)(2,1)} fusion(bf16[128,32,512]{2,1,0:T(8,128)(2,1)} %bitcast.47, pred[128,32]{1,0:T(8,128)(4,1)S(1)} %copy.15), kind=kLoop, calls=%fused_computation.41 | loop fusion | flops 2097152 | bytes 8392704 | tf_op jit(solution)/shard_map/jit(_take)/select_n | solution.py:39
  175.2 0.0 copy-start.5
  175.2 0.0 copy-start.6
  175.2 10.5 %all-to-all-start = ((bf16[128,32,512]{2,1,0:T(8,128)(2,1)}), bf16[128,32,512]{2,1,0:T(8,128)(2,1)}, u32[]{:S(2)}, u32[]{:S(2)}) async-start(bf16[128,32,512]{2,1,0:T(8,128)(2,1)} %broadcast_select_fusion), calls=%async_computation.1 | async-start | bytes 8388608 | tf_op jit(solution)/shard_map/all_to_all | solution.py:40
  185.8 0.0 copy-done.5
  185.8 0.0 copy-done.6
  185.8 50.4 %all-to-all-done = bf16[128,32,512]{2,1,0:T(8,128)(2,1)} async-done(((bf16[128,32,512]{2,1,0:T(8,128)(2,1)}), bf16[128,32,512]{2,1,0:T(8,128)(2,1)}, u32[]{:S(2)}, u32[]{:S(2)}) %all-to-all-start) | async-done | bytes 4194336 | tf_op jit(solution)/shard_map/all_to_all | solution.py:40
  236.2 0.0 copy-done.1
  236.2 0.0 copy-start.3
  236.2 0.0 copy-start.8
  236.2 0.0 copy-start.9
  236.2 4.9 %pad_maximum_fusion = bf16[5120,512]{1,0:T(8,128)(2,1)} fusion(bf16[4096,512]{1,0:T(8,128)(2,1)} %bitcast.8, bf16[1024,512]{1,0:T(8,128)(2,1)S(1)} %fusion.34), kind=kLoop, calls=%fused_computation.39 | loop fusion | flops 10485760 | bytes 10485760 | tf_op jit(solution)/shard_map/concatenate | solution.py:41
  241.1 0.0 copy-done.3
  241.1 0.0 copy-done.8
  241.1 0.0 copy-done.9
  241.1 91.3 %while.10 = (s32[]{:T(128)}, f32[4,1024,128]{2,1,0:T(8,128)}, s32[4,1024]{1,0:T(4,128)S(1)}, bf16[5120,512]{1,0:T(8,128)(2,1)}, bf16[512,2048]{1,0:T(8,128)(2,1)...) while((s32[]{:T(128)}, f32[4,1024,128]{2,1,0:T(8,128)}, ...), condition=%wide.region_4.5_spmd, body=%wide.region_3.4_spmd.sunk | while | flops 4050167808 | bytes 49327220 | solution.py:59
  241.2 7.2 %gather_fusion = bf16[1024,512]{1,0:T(8,128)(2,1)S(1)} fusion(bf16[5120,512]{1,0:T(8,128)(2,1)} %get-tuple-element.167, s32[1024]{0:T(1024)S(1)} %broadcast_clamp_fusion.3), kind=kCustom, calls=%fused_computation.clone.1 | custom fusion | bytes 2101248 | tf_op jit(solution)/shard_map/while/body/eval_jaxpr/jit(_take)/gather | solution.py:49
  248.3 4.0 %fusion.67 = f32[1024,2048]{1,0:T(8,128)S(1)} fusion(bf16[512,2048]{1,0:T(8,128)(2,1)} %get-tuple-element.168, bf16[1024,512]{1,0:T(8,128)(2,1)S(1)} %gather_fusion, pred[1024]{0:T(1024)(128)(4,1)S(1)} %compare_and_fusion.3), kind=kOutput, calls=%fused_computation.13.clone.1 | convolution fusion | flops 2148007936 | bytes 11535360 | tf_op jit(solution)/shard_map/while/body/eval_jaxpr/dot_general | solution.py:50
  252.3 2.2 fusion.68
  254.5 7.4 %fusion.69 = bf16[1024,2048]{1,0:T(8,128)(2,1)S(1)} fusion(f32[1024,2048]{1,0:T(8,128)S(1)} %fusion.67, f32[1024,2048]{1,0:T(8,128)S(1)} %fusion.68, f32[32,2048]{1,0:T(8,128)S(1)} %get-tuple-element.172, s32[1024]{0:T(1024)S(1)} %bitcast.51), kind=kOutput, calls=%fused_computation.10.clone.1 | convolution fusion | flops 828407808 | bytes 21237760 | tf_op jit(solution)/shard_map/while/body/eval_jaxpr/dot_general | solution.py:55
  261.9 2.0 fusion.70
  264.0 7.2 %gather_fusion = bf16[1024,512]{1,0:T(8,128)(2,1)S(1)} fusion(bf16[5120,512]{1,0:T(8,128)(2,1)} %get-tuple-element.167, s32[1024]{0:T(1024)S(1)} %broadcast_clamp_fusion.3), kind=kCustom, calls=%fused_computation.clone.1 | custom fusion | bytes 2101248 | tf_op jit(solution)/shard_map/while/body/eval_jaxpr/jit(_take)/gather | solution.py:49
  271.1 4.0 %fusion.67 = f32[1024,2048]{1,0:T(8,128)S(1)} fusion(bf16[512,2048]{1,0:T(8,128)(2,1)} %get-tuple-element.168, bf16[1024,512]{1,0:T(8,128)(2,1)S(1)} %gather_fusion, pred[1024]{0:T(1024)(128)(4,1)S(1)} %compare_and_fusion.3), kind=kOutput, calls=%fused_computation.13.clone.1 | convolution fusion | flops 2148007936 | bytes 11535360 | tf_op jit(solution)/shard_map/while/body/eval_jaxpr/dot_general | solution.py:50
  275.1 2.2 fusion.68
  277.4 7.4 %fusion.69 = bf16[1024,2048]{1,0:T(8,128)(2,1)S(1)} fusion(f32[1024,2048]{1,0:T(8,128)S(1)} %fusion.67, f32[1024,2048]{1,0:T(8,128)S(1)} %fusion.68, f32[32,2048]{1,0:T(8,128)S(1)} %get-tuple-element.172, s32[1024]{0:T(1024)S(1)} %bitcast.51), kind=kOutput, calls=%fused_computation.10.clone.1 | convolution fusion | flops 828407808 | bytes 21237760 | tf_op jit(solution)/shard_map/while/body/eval_jaxpr/dot_general | solution.py:55
  284.7 2.0 fusion.70
  286.8 7.2 %gather_fusion = bf16[1024,512]{1,0:T(8,128)(2,1)S(1)} fusion(bf16[5120,512]{1,0:T(8,128)(2,1)} %get-tuple-element.167, s32[1024]{0:T(1024)S(1)} %broadcast_clamp_fusion.3), kind=kCustom, calls=%fused_computation.clone.1 | custom fusion | bytes 2101248 | tf_op jit(solution)/shard_map/while/body/eval_jaxpr/jit(_take)/gather | solution.py:49
  294.0 4.0 %fusion.67 = f32[1024,2048]{1,0:T(8,128)S(1)} fusion(bf16[512,2048]{1,0:T(8,128)(2,1)} %get-tuple-element.168, bf16[1024,512]{1,0:T(8,128)(2,1)S(1)} %gather_fusion, pred[1024]{0:T(1024)(128)(4,1)S(1)} %compare_and_fusion.3), kind=kOutput, calls=%fused_computation.13.clone.1 | convolution fusion | flops 2148007936 | bytes 11535360 | tf_op jit(solution)/shard_map/while/body/eval_jaxpr/dot_general | solution.py:50
  297.9 2.2 fusion.68
  300.2 7.4 %fusion.69 = bf16[1024,2048]{1,0:T(8,128)(2,1)S(1)} fusion(f32[1024,2048]{1,0:T(8,128)S(1)} %fusion.67, f32[1024,2048]{1,0:T(8,128)S(1)} %fusion.68, f32[32,2048]{1,0:T(8,128)S(1)} %get-tuple-element.172, s32[1024]{0:T(1024)S(1)} %bitcast.51), kind=kOutput, calls=%fused_computation.10.clone.1 | convolution fusion | flops 828407808 | bytes 21237760 | tf_op jit(solution)/shard_map/while/body/eval_jaxpr/dot_general | solution.py:55
  307.5 2.0 fusion.70
  309.6 7.2 %gather_fusion = bf16[1024,512]{1,0:T(8,128)(2,1)S(1)} fusion(bf16[5120,512]{1,0:T(8,128)(2,1)} %get-tuple-element.167, s32[1024]{0:T(1024)S(1)} %broadcast_clamp_fusion.3), kind=kCustom, calls=%fused_computation.clone.1 | custom fusion | bytes 2101248 | tf_op jit(solution)/shard_map/while/body/eval_jaxpr/jit(_take)/gather | solution.py:49
  316.8 4.0 %fusion.67 = f32[1024,2048]{1,0:T(8,128)S(1)} fusion(bf16[512,2048]{1,0:T(8,128)(2,1)} %get-tuple-element.168, bf16[1024,512]{1,0:T(8,128)(2,1)S(1)} %gather_fusion, pred[1024]{0:T(1024)(128)(4,1)S(1)} %compare_and_fusion.3), kind=kOutput, calls=%fused_computation.13.clone.1 | convolution fusion | flops 2148007936 | bytes 11535360 | tf_op jit(solution)/shard_map/while/body/eval_jaxpr/dot_general | solution.py:50
  320.8 2.2 fusion.68
  323.0 7.4 %fusion.69 = bf16[1024,2048]{1,0:T(8,128)(2,1)S(1)} fusion(f32[1024,2048]{1,0:T(8,128)S(1)} %fusion.67, f32[1024,2048]{1,0:T(8,128)S(1)} %fusion.68, f32[32,2048]{1,0:T(8,128)S(1)} %get-tuple-element.172, s32[1024]{0:T(1024)S(1)} %bitcast.51), kind=kOutput, calls=%fused_computation.10.clone.1 | convolution fusion | flops 828407808 | bytes 21237760 | tf_op jit(solution)/shard_map/while/body/eval_jaxpr/dot_general | solution.py:55
  330.3 2.0 fusion.70
  (24 shorter events, 0.2 us)
Async XLA Ops:
  7.2 54.8 %copy-start = (bf16[512,512]{1,0:T(8,128)(2,1)S(1)}, bf16[512,512]{1,0:T(8,128)(2,1)}, u32[]{:S(2)}) copy-start(bf16[512,512]{1,0:T(8,128)(2,1)} %param.17) | copy-start | bytes 1572868
  7.2 54.8 %copy-start.7 = (bf16[512,512]{1,0:T(8,128)(2,1)S(1)}, bf16[512,512]{1,0:T(8,128)(2,1)}, u32[]{:S(2)}) copy-start(bf16[512,512]{1,0:T(8,128)(2,1)} %param.16) | copy-start | bytes 1572868
  7.2 54.8 %all-gather.2.cloned.1.call-start = ((), (), s32[]{:S(2)}) async-start(), calls=%async_computation.2 | async-start | bytes 5242880 | tf_op jit(solution)/shard_map/all_gather | solution.py:31
  13.1 138.9 %reduce-scatter.2.cloned.1.call-start = ((), (), s32[]{:S(2)}) async-start(), calls=%async_computation.3 | async-start | bytes 10485760 | tf_op jit(solution)/shard_map/reduce_scatter | solution.py:37
  71.2 0.7 copy-start.4
  71.2 80.8 %copy-start.2 = (bf16[1024,512]{1,0:T(8,128)(2,1)S(1)}, bf16[1024,512]{1,0:T(8,128)(2,1)}, u32[]{:S(2)}) copy-start(bf16[1024,512]{1,0:T(8,128)(2,1)} %param.14) | copy-start | bytes 3145732
  154.0 82.2 %copy-start.1 = (bf16[1024,512]{1,0:T(8,128)(2,1)}, bf16[1024,512]{1,0:T(8,128)(2,1)S(1)}, u32[]{:S(2)}) copy-start(bf16[1024,512]{1,0:T(8,128)(2,1)S(1)} %fusion.34) | copy-start | bytes 3145732
  175.2 10.5 %copy-start.5 = (s32[4096]{0:T(1024)S(1)}, s32[4096]{0:T(1024)}, u32[]{:S(2)}) copy-start(s32[4096]{0:T(1024)} %param.19) | copy-start | bytes 49156
  175.2 10.6 %copy-start.6 = (s32[4096]{0:T(1024)S(1)}, s32[4096]{0:T(1024)}, u32[]{:S(2)}) copy-start(s32[4096]{0:T(1024)} %param.21) | copy-start | bytes 49156
  175.2 60.9 %all-to-all-start = ((bf16[128,32,512]{2,1,0:T(8,128)(2,1)}), bf16[128,32,512]{2,1,0:T(8,128)(2,1)}, u32[]{:S(2)}, u32[]{:S(2)}) async-start(bf16[128,32,512]{2,1,0:T(8,128)(2,1)} %broadcast_select_fusion), calls=%async_computation.1 | async-start | bytes 8388608 | tf_op jit(solution)/shard_map/all_to_all | solution.py:40
  236.2 4.9 %copy-start.3 = (bf16[128,2048]{1,0:T(8,128)(2,1)S(1)}, bf16[128,2048]{1,0:T(8,128)(2,1)}, u32[]{:S(2)}) copy-start(bf16[128,2048]{1,0:T(8,128)(2,1)} %param.24) | copy-start | bytes 1572868
  236.2 4.9 %copy-start.8 = (bf16[2048,128]{1,0:T(8,128)(2,1)S(1)}, bf16[2048,128]{1,0:T(8,128)(2,1)}, u32[]{:S(2)}) copy-start(bf16[2048,128]{1,0:T(8,128)(2,1)} %param.25) | copy-start | bytes 1572868
  236.2 4.9 %copy-start.9 = (f32[32,2048]{1,0:T(8,128)S(1)}, f32[32,2048]{1,0:T(8,128)}, u32[]{:S(2)}) copy-start(f32[32,2048]{1,0:T(8,128)} %param.22) | copy-start | bytes 786436
Sparse Core Ops, SparseCore 0:
  13.2 48.7 all-gather.1
  71.4 80.6 reduce-scatter.1
where the time goes:
time: 344 us; the launch traced here: 339 us
  waiting for transfers between devices  179 us (52%)
  matrix products  71.5 us (21%)
  local copies, waits for them, and re-layouts  47 us (14%)
  other arithmetic  16.7 us (5%)
  between operations  14.2 us (4%)
  starting transfers between devices  10.6 us (3%)
    reduce_scatter x1, waiting for transfers between devices, local(): update = lax.psum_scatter(partials, 'tp', scatter_dimension=0, tiled=True)  79.7 us
    all_to_all x1, waiting for transfers between devices, local(): lax.all_to_all(outgoing, ('pix', 'tp'), split_axis=0, concat_axis=0, tile...  50.4 us
    all_gather x1, waiting for transfers between devices, local(): lax.all_gather(normed, 'tp', axis=0, tiled=True)  48.8 us
    dot_general x4, matrix products, decode_block(): pre = pre + jnp.dot(one_hot, inst_embed, precision=lax.Precision.HIGHEST)  29.4 us
    gather x4, local copies, waits for them, and re-layouts, decode_block(): gathered = jnp.take(table, sources, axis=0)  28.6 us
    gather x1, local copies, waits for them, and re-layouts, local(): outgoing = jnp.take(updated, send_rows.reshape(-1), axis=0)  17.3 us
    dot_general x4, matrix products, decode_block(): pre = jnp.dot(gathered, w_dec, preferred_element_type=jnp.float32)  15.9 us
    all_to_all x1, starting transfers between devices, local(): lax.all_to_all(outgoing, ('pix', 'tp'), split_axis=0, concat_axis=0, tile...  10.5 us
  transfers between devices with their start and end apart: 3, of which 3 were waited for; matrix products, arithmetic and copies ran while one was open for 0% of the time, Pallas kernels for 0%

commit v1 on v0

v1 whole, which is shorter than its diff:
```python
import functools

import jax
import jax.numpy as jnp
from jax import lax
from jax.experimental import pallas as pl
from jax.experimental.pallas import tpu as pltpu
from jax.sharding import PartitionSpec as P

MESH = pl.DeviceIdType.MESH
F32, BF16 = jnp.float32, jnp.bfloat16

ROWS = 1024
D = 512
FF = 2048
CAP = 32
NDEV = 128
PER = 8
CHUNKS = NDEV // PER
CROWS = PER * CAP
RAW = 8
MUL, INV = 37, 45
BLOCK = 512
OBS = 4096


def gelu(x):
    u = x * (0.7978845608028654 + 0.035677408136300125 * (x * x))
    h = 0.5 * x
    return h + h * jnp.tanh(u)


def coords():
    p, y = lax.axis_index("pix"), lax.axis_index("tp")
    return p // 8, (p // 2) % 4, p % 2, y


def partner(k):
    x, z, c, y = coords()
    kk = (MUL * k) % NDEV
    dy, dc, dz, dx = kk % 4, (kk // 4) % 2, (kk // 8) % 4, kk // 32
    return ((x + dx) % 4) * 8 + ((z + dz) % 4) * 2 + (c + dc) % 2, (y + dy) % 4


def process(rows, gain, w_ref):
    values = rows.astype(F32)
    center = values - jnp.mean(values, axis=-1, keepdims=True)
    spread = jnp.mean(center * center, axis=-1, keepdims=True)
    normed = (center * lax.rsqrt(spread + 1e-05) * gain).astype(BF16)
    acc = values
    for d in range(4):
        inner = gelu(jnp.dot(normed, w_ref[d, 0].reshape(D, D), preferred_element_type=F32)).astype(BF16)
        acc = acc + jnp.dot(inner, w_ref[d, 1].reshape(D, D), preferred_element_type=F32)
    return acc.astype(BF16)


def exchange_kernel(
    latent, gain, w_in, w_out, send_rows, obs_src, table, index,
    w, send, raw, upd, ids, load_sem, w_send, w_recv, send_sem, recv_sem, out_sem, s2, s3, s4,
):
    x, z, c, y = coords()
    pix = lax.axis_index("pix")
    sib = pix + 1 - 2 * c
    xs = [(((x + d) % 4) * 8 + z * 2 + c, y) for d in (1, 2, 3)]
    zs = [(x * 8 + ((z + d) % 4) * 2 + c, y) for d in (1, 2, 3)]
    ys = [(pix, (y + 4 - d) % 4) for d in (1, 2, 3)]

    def signal(sem, who):
        for dev in who:
            pl.semaphore_signal(sem, inc=1, device_id=dev, device_id_type=MESH)

    barrier = pltpu.get_barrier_semaphore()
    signal(barrier, ys + zs + xs + [(sib, y)])
    loads = [
        pltpu.make_async_copy(w_in, w.at[0, 0], load_sem.at[0]),
        pltpu.make_async_copy(w_out, w.at[0, 1], load_sem.at[1]),
    ]
    for load in loads:
        load.start()

    ids[...] = jnp.concatenate(
        [send_rows[...].astype(F32), jnp.zeros((NDEV, NDEV - CAP), F32)], axis=1
    ).T[:CAP]

    r = obs_src[...]
    s = jnp.maximum(r - ROWS, 0) // CAP
    sp, st = s // 4, s % 4
    kk = (
        (y - st + 4) % 4
        + 4 * ((c - sp % 2 + 2) % 2)
        + 8 * ((z - (sp // 2) % 4 + 4) % 4)
        + 32 * ((x - sp // 8 + 4) % 4)
    )
    index[...] = jnp.where(r < ROWS, r, ROWS + ((INV * kk) % NDEV) * CAP + (r - ROWS) % CAP)

    pl.semaphore_wait(barrier, 10)
    signal(s2, zs)
    for load in loads:
        load.wait()

    pieces = (c * 8 + x, c * 8 + 4 + z)
    for d, dev in zip((1, 2, 3), ys):
        for piece in pieces:
            pltpu.make_async_remote_copy(
                w.at[0, :, piece], w.at[d, :, piece], w_send, w_recv.at[0], device_id=dev, device_id_type=MESH
            ).start()

    lane = lax.broadcasted_iota(jnp.int32, (CAP, NDEV), 1)
    cell = lax.broadcasted_iota(jnp.int32, (CAP, ROWS), 1)

    def gather(j, source):
        def hot(i):
            pp, tt = partner(j * PER + i)
            column = jnp.sum(jnp.where(lane == pp * 4 + tt, ids[...], 0.0), axis=1, keepdims=True)
            return jnp.where(cell == column.astype(jnp.int32), 1.0, 0.0).astype(BF16)

        picked = jnp.concatenate([hot(i) for i in range(PER)], axis=0)
        rows = jnp.dot(picked, source[...], preferred_element_type=F32).astype(BF16)
        send[pl.ds(j * PER, PER)] = rows.reshape(PER, CAP, D)

    def to_raw(k):
        pp, tt = partner(k)
        pltpu.make_async_remote_copy(
            send.at[k], raw.at[k], send_sem, recv_sem.at[k // PER], device_id=(pp, tt), device_id_type=MESH
        ).start()

    def to_table(k):
        pp, tt = partner(k)
        pltpu.make_async_remote_copy(
            send.at[k], table.at[pl.ds(pl.multiple_of(ROWS + k * CAP, CAP), CAP)],
            send_sem, recv_sem.at[k // PER], device_id=(pp, tt), device_id_type=MESH,
        ).start()

    def start(j, put):
        def one(i, _):
            put(j * PER + i)
            return 0

        lax.fori_loop(0, PER, one, 0)

    def raw_chunks(lo, hi):
        def one(j, _):
            gather(j, latent)
            start(j, to_raw)
            return 0

        lax.fori_loop(lo, hi, one, 0)

    gather(0, latent)
    pl.semaphore_wait(s2, 3)
    signal(s3, xs)
    gather(1, latent)
    raw[0] = send[0]
    pl.semaphore_wait(s3, 3)
    signal(s4, [(sib, y)])
    gather(2, latent)
    pl.semaphore_wait(s4, 1)

    def first(k, _):
        to_raw(k)
        return 0

    lax.fori_loop(1, 3 * PER, first, 0)

    pltpu.make_async_copy(w.at[pl.ds(1, 3), :, pl.ds(0, 2)], w.at[pl.ds(1, 3), :, pl.ds(0, 2)], w_recv.at[0]).wait()
    for piece, line in zip(pieces, (xs, zs)):
        for dev in line:
            part = w.at[pl.ds(1, 3), :, piece]
            pltpu.make_async_remote_copy(part, part, w_send, w_recv.at[1], device_id=dev, device_id_type=MESH).start()
    raw_chunks(3, 6)
    pltpu.make_async_copy(w.at[pl.ds(1, 3), :, pl.ds(0, 6)], w.at[pl.ds(1, 3), :, pl.ds(0, 6)], w_recv.at[1]).wait()
    half = w.at[pl.ds(1, 3), :, pl.ds(c * 8, 8)]
    pltpu.make_async_remote_copy(half, half, w_send, w_recv.at[2], device_id=(sib, y), device_id_type=MESH).start()
    raw_chunks(6, RAW)
    pltpu.make_async_copy(w.at[pl.ds(1, 3), :, pl.ds(0, 8)], w.at[pl.ds(1, 3), :, pl.ds(0, 8)], w_recv.at[2]).wait()

    def own(i, _):
        at = pl.ds(pl.multiple_of(i * CROWS, CROWS), CROWS)
        upd[at] = process(latent[at], gain[...], w)
        return 0

    lax.fori_loop(0, ROWS // CROWS, own, 0)
    keep = pltpu.make_async_copy(upd, table.at[pl.ds(0, ROWS)], out_sem.at[0])
    keep.start()

    def processed(j, _):
        gather(j, upd)
        start(j, to_table)
        return 0

    lax.fori_loop(RAW, CHUNKS, processed, 0)

    def arrived(j, _):
        @pl.when(j == 0)
        def _():
            pltpu.make_async_copy(raw.at[pl.ds(1, PER - 1)], raw.at[pl.ds(1, PER - 1)], recv_sem.at[0]).wait()

        @pl.when(j > 0)
        def _():
            part = raw.at[pl.ds(j * PER, PER)]
            pltpu.make_async_copy(part, part, recv_sem.at[j]).wait()

        at = pl.ds(j * PER, PER)
        raw[at] = process(raw[at].reshape(CROWS, D), gain[...], w).reshape(PER, CAP, D)
        return 0

    lax.fori_loop(0, RAW, arrived, 0)
    outs = pltpu.make_async_copy(
        raw, table.at[pl.ds(ROWS, RAW * CROWS)].reshape(RAW * PER, CAP, D), out_sem.at[1]
    )
    outs.start()

    def late(j, _):
        part = table.at[pl.ds(pl.multiple_of(ROWS + j * CROWS, CROWS), CROWS)]
        pltpu.make_async_copy(part, part, recv_sem.at[j]).wait()
        return 0

    lax.fori_loop(RAW, CHUNKS, late, 0)
    keep.wait()
    outs.wait()
    pltpu.make_async_copy(send.at[pl.ds(0, NDEV - 1)], send.at[pl.ds(0, NDEV - 1)], send_sem).wait()
    for n in (2, 6, 8):
        part = w.at[pl.ds(1, 3), :, pl.ds(0, n)]
        pltpu.make_async_copy(part, part, w_send).wait()


def exchange(latent, gain, w_in, w_out, send_rows, obs_src):
    vmem, any_ = pl.BlockSpec(memory_space=pltpu.VMEM), pl.BlockSpec(memory_space=pl.ANY)
    return pl.pallas_call(
        exchange_kernel,
        out_shape=(
            jax.ShapeDtypeStruct((ROWS + NDEV * CAP, D), BF16),
            jax.ShapeDtypeStruct((OBS // 128, 128), jnp.int32),
        ),
        in_specs=[vmem, vmem, any_, any_, vmem, vmem],
        out_specs=(any_, vmem),
        scratch_shapes=[
            pltpu.VMEM((4, 2, 16, 32, D), BF16),
            pltpu.VMEM((NDEV, CAP, D), BF16),
            pltpu.VMEM((RAW * PER, CAP, D), BF16),
            pltpu.VMEM((ROWS, D), BF16),
            pltpu.VMEM((CAP, NDEV), F32),
            pltpu.SemaphoreType.DMA((2,)),
            pltpu.SemaphoreType.DMA,
            pltpu.SemaphoreType.DMA((3,)),
            pltpu.SemaphoreType.DMA,
            pltpu.SemaphoreType.DMA((CHUNKS,)),
            pltpu.SemaphoreType.DMA((2,)),
            pltpu.SemaphoreType.REGULAR,
            pltpu.SemaphoreType.REGULAR,
            pltpu.SemaphoreType.REGULAR,
        ],
        compiler_params=pltpu.CompilerParams(collective_id=0, has_side_effects=True, vmem_limit_bytes=56 << 20),
        name="exchange",
    )(latent, gain.reshape(1, D), w_in.reshape(16, 32, D), w_out.reshape(16, 32, D), send_rows, obs_src.reshape(OBS // 128, 128))


def decode_kernel(
    index, table, feat, inst, embed, w_dec, w_feat, w_head, latent_out, decoded, tab, picked, w2, sem
):
    step = pl.program_id(0)
    keep = pltpu.make_async_copy(table.at[pl.ds(0, ROWS)], latent_out, sem)

    @pl.when(step == 0)
    def _():
        keep.start()

        def widen(i, _):
            for n in range(4):
                at = pl.ds(pl.multiple_of(i * 256, 256), 256)
                tab[pl.ds(i * 1024 + n, 256, stride=4), :] = table[at, n * 128:(n + 1) * 128].astype(F32)
            return 0

        lax.fori_loop(0, (ROWS + NDEV * CAP) // 256, widen, 0)
        high = embed[...].astype(BF16)
        w2[0:128] = w_feat[...]
        w2[128:160] = high
        w2[160:192] = (embed[...] - high.astype(F32)).astype(BF16)

    def pick(i, _):
        for u in range(16):
            j = i * 16 + u
            row = index[step * BLOCK + j]
            picked[pl.ds(pl.multiple_of(j * 4, 4), 4), :] = tab[pl.ds(pl.multiple_of(row * 4, 4), 4), :]
        return 0

    lax.fori_loop(0, BLOCK // 16, pick, 0)
    rows = jnp.concatenate([picked[pl.ds(n, BLOCK, stride=4), :].astype(BF16) for n in range(4)], axis=1)
    which = lax.broadcasted_iota(jnp.int32, (64, BLOCK), 0) % 32
    hot = jnp.where(which == inst[0], 1.0, 0.0).T.astype(BF16)
    side = jnp.concatenate([feat[...], hot], axis=1)
    total = jnp.zeros((BLOCK, 128), F32)
    for n in range(4):
        at = slice(n * 512, (n + 1) * 512)
        pre = jnp.dot(rows, w_dec[:, at], preferred_element_type=F32) + jnp.dot(
            side, w2[:, at], preferred_element_type=F32
        )
        total = total + jnp.dot(gelu(pre).astype(BF16), w_head[at, :], preferred_element_type=F32)
    decoded[...] = total

    @pl.when(step == OBS // BLOCK - 1)
    def _():
        keep.wait()


def decode(index, table, feat, inst, embed, w_dec, w_feat, w_head):
    whole = lambda a: pl.BlockSpec(a.shape, lambda i, _: (0, 0), pipeline_mode=pl.Buffered(1))
    return pl.pallas_call(
        decode_kernel,
        out_shape=(jax.ShapeDtypeStruct((ROWS, D), BF16), jax.ShapeDtypeStruct((OBS, 128), F32)),
        grid_spec=pltpu.PrefetchScalarGridSpec(
            num_scalar_prefetch=1,
            grid=(OBS // BLOCK,),
            in_specs=[
                whole(table),
                pl.BlockSpec((BLOCK, 128), lambda i, _: (i, 0)),
                pl.BlockSpec((1, 1, BLOCK), lambda i, _: (i, 0, 0)),
                whole(embed), whole(w_dec), whole(w_feat), whole(w_head),
            ],
            out_specs=(pl.BlockSpec(memory_space=pl.ANY), pl.BlockSpec((BLOCK, 128), lambda i, _: (i, 0))),
            scratch_shapes=[
                pltpu.VMEM((4 * (ROWS + NDEV * CAP), 128), F32),
                pltpu.VMEM((4 * BLOCK, 128), F32),
                pltpu.VMEM((192, FF), BF16),
                pltpu.SemaphoreType.DMA,
            ],
        ),
        compiler_params=pltpu.CompilerParams(vmem_limit_bytes=56 << 20, dimension_semantics=("arbitrary",)),
        name="decode",
    )(index, table, feat, inst.reshape(OBS // BLOCK, 1, BLOCK), embed, w_dec, w_feat, w_head)


def local(latent, norm_gain, w_in, w_out, send_rows, obs_src, obs_feat, obs_inst, inst_embed, w_dec, w_feat, w_head):
    table, index = exchange(latent, norm_gain, w_in, w_out, send_rows, obs_src)
    return decode(index.reshape(-1), table, obs_feat, obs_inst, inst_embed, w_dec, w_feat, w_head)


def solution(mesh):
    in_specs = (
        P(("pix", "tp"), None),
        P(),
        P(None, "tp"),
        P("tp", None),
        P(("pix", "tp"), None),
        P(("pix", "tp")),
        P(("pix", "tp"), None),
        P(("pix", "tp")),
        P(),
        P(),
        P(),
        P(),
    )
    out_specs = (P(("pix", "tp"), None), P(("pix", "tp"), None))
    return jax.shard_map(local, mesh=mesh, in_specs=in_specs, out_specs=out_specs, check_vma=False)
```

time: 344 us -> 123 us (0.36)
  the two profiles are of different devices: /device:TPU:27 before, /device:TPU:18 now
where the time goes in v1:
time: 123 us
  Pallas kernels  121 us (98%)
  local copies, waits for them, and re-layouts  1.45 us (1%)
    pallas_call x1, Pallas kernels, exchange(): pl.pallas_call(exchange_kernel, out_shape=(jax.ShapeDtypeStruct((ROWS + N...  84.8 us
    pallas_call x1, Pallas kernels, decode(): pl.pallas_call(decode_kernel, out_shape=(jax.ShapeDtypeStruct((ROWS, D),...  36.1 us

profile of v1, /device:TPU:18, one launch (start us, length us, event | category | flops | bytes accessed | tf_op | source)
XLA Modules:
  0.0 123.0 jit_solution(2625780975716205651)
XLA Ops:
  0.6 1.4 %copy.14.send_rows = s32[128,32]{1,0:T(8,128)} copy(s32[128,32]{0,1:T(8,128)} %param.16) | data formatting | bytes 32768 | tf_op args[4]
  2.1 84.8 %exchange.1 = (bf16[5120,512]{1,0:T(8,128)(2,1)}, s32[32,128]{1,0:T(8,128)}) custom-call(bf16[1024,512]{1,0:T(8,128)(2,1)} %latent.1, f32[1,512]{1,0:T(1,128)} %bitcast.11, bf16[16,32,512]{2,1,0:T(8,128)(2,1)} %bitcast.6, bf16[16,32,512]{2,1,0:T(8,128)(2,1)} %bitcast.7, s32[128,32]{1,0:T(8,128)} %copy.14.send_rows, s32[32,128]{1,0:T(8,128)} %bitcast.8), custom_call_target="tpu_custom_call" | custom-call | tf_op jit(solution)/shard_map/exchange/pallas_call | solution.py:229
  86.9 36.1 %decode.1 = (bf16[1024,512]{1,0:T(8,128)(2,1)}, f32[4096,128]{1,0:T(8,128)}) custom-call(s32[4096]{0:T(1024)} %bitcast.10, bf16[5120,512]{1,0:T(8,128)(2,1)} %get-tuple-element.5.table, bf16[4096,128]{1,0:T(8,128)(2,1)} %feat.1, s32[8,1,512]{2,1,0:T(1,128)} %bitcast.9, f32[32,2048]{1,0:T(8,128)} %embed.1, bf16[512,2048]{1,0:T(8,128)(2,1)} %w_dec.1, ...), custom_call_target="tpu_custom_call" | custom-call | tf_op jit(solution)/shard_map/decode/pallas_call | solution.py:308

commit v2 on v0

v2 whole, which is shorter than its diff:
```python
import jax
import jax.numpy as jnp
from jax import lax
from jax.experimental import pallas as pl
from jax.experimental.pallas import tpu as pltpu
from jax.sharding import PartitionSpec as P

MESH = pl.DeviceIdType.MESH
F32, BF16 = jnp.float32, jnp.bfloat16

ROWS = 1024
D = 512
FF = 2048
CAP = 32
NDEV = 128
PER = 8
CHUNKS = NDEV // PER
CROWS = PER * CAP
MUL, INV = 37, 45
TABLE = ROWS + NDEV * CAP
OBS = 4096
BLOCK = 512
BLOCKS = OBS // BLOCK
EVENTS = CHUNKS + 1
SIDE = 192


def gelu(x):
    u = x * (0.7978845608028654 + 0.035677408136300125 * (x * x))
    h = 0.5 * x
    return h + h * jnp.tanh(u)


def coords():
    p, y = lax.axis_index("pix"), lax.axis_index("tp")
    return p // 8, (p // 2) % 4, p % 2, y


def partner(k):
    x, z, c, y = coords()
    kk = (MUL * k) % NDEV
    dy, dc, dz, dx = kk % 4, (kk // 4) % 2, (kk // 8) % 4, kk // 32
    return ((x + dx) % 4) * 8 + ((z + dz) % 4) * 2 + (c + dc) % 2, (y + dy) % 4


def step_of(block):
    return (5 * block) // 2


def process(rows, gain, wi, wo, inner):
    values = rows.astype(F32)
    center = values - jnp.mean(values, axis=-1, keepdims=True)
    spread = jnp.mean(center * center, axis=-1, keepdims=True)
    normed = (center * lax.rsqrt(spread + 1e-05) * gain).astype(BF16)
    for d in range(4):
        inner[:, d * D:(d + 1) * D] = gelu(
            jnp.dot(normed, wi[d].reshape(D, D), preferred_element_type=F32)
        ).astype(BF16)
    update = jnp.dot(inner[...], wo[...].reshape(FF, D), preferred_element_type=F32)
    return (values + update).astype(BF16)


def widen(tab, start, rows):
    n = rows.shape[0]
    for q in range(4):
        tab[pl.ds(start * 4 + q, n, stride=4), :] = rows[:, q * 128:(q + 1) * 128].astype(F32)


def load_decoder(embed, wall):
    high = embed[...].astype(BF16)
    wall[640:672] = high
    wall[672:704] = (embed[...] - high.astype(F32)).astype(BF16)


def pick_sides(order_s, order_v, feats, sorted_feats, sides):
    def pick(i, _):
        for u in range(16):
            j = i * 16 + u
            sorted_feats[pl.ds(j, 1), :] = feats[pl.ds(order_s[OBS + j], 1), :]
        return 0

    lax.fori_loop(0, OBS // 16, pick, 0)
    which = lax.broadcasted_iota(jnp.int32, (64, BLOCK), 0) % 32

    def fill(b, _):
        at = pl.ds(pl.multiple_of(b * BLOCK, BLOCK), BLOCK)
        inst = order_v[pl.ds(64 + b * (BLOCK // 128), BLOCK // 128), :]
        inst = jnp.concatenate([inst[q:q + 1] for q in range(BLOCK // 128)], axis=1)
        hot = jnp.where(which == inst, 1.0, 0.0).T.astype(BF16)
        sides[at] = jnp.concatenate([sorted_feats[at].astype(BF16), hot], axis=1)
        return 0

    lax.fori_loop(0, BLOCKS, fill, 0)


def decode_block(b, order_s, tab, picked, sides, wall, hidden, head):
    at = pl.ds(pl.multiple_of(b * BLOCK, BLOCK), BLOCK)

    def pick(i, _):
        for u in range(16):
            j = i * 16 + u
            picked[pl.ds(pl.multiple_of(j * 4, 4), 4), :] = tab[pl.ds(order_s[b * BLOCK + j] * 4, 4), :]
        return 0

    lax.fori_loop(0, BLOCK // 16, pick, 0)
    full = jnp.concatenate(
        [picked[pl.ds(q, BLOCK, stride=4), :].astype(BF16) for q in range(4)] + [sides[at]], axis=1
    )
    for n in range(4):
        cols = slice(n * 512, (n + 1) * 512)
        hidden[:, cols] = gelu(jnp.dot(full, wall[:, cols], preferred_element_type=F32)).astype(BF16)
    return jnp.dot(hidden[...], head[...], preferred_element_type=F32)


def lines():
    x, z, c, y = coords()
    xs = [(((x + d) % 4) * 8 + z * 2 + c, y) for d in (1, 2, 3)]
    zs = [(x * 8 + ((z + d) % 4) * 2 + c, y) for d in (1, 2, 3)]
    ys = [(x * 8 + z * 2 + c, (y + 4 - d) % 4) for d in (1, 2, 3)]
    return xs, ys, zs, [(x * 8 + z * 2 + 1 - c, y)]


def signal(sem, who):
    for dev in who:
        pl.semaphore_signal(sem, inc=1, device_id=dev, device_id_type=MESH)


def sort(obs_src, obs_inst, order, acc):
    x, z, c, y = coords()
    r = obs_src[...]
    s = jnp.maximum(r - ROWS, 0) // CAP
    sp, st = s // 4, s % 4
    kk = (
        (y - st + 4) % 4
        + 4 * ((c - sp % 2 + 2) % 2)
        + 8 * ((z - (sp // 2) % 4 + 4) % 4)
        + 32 * ((x - sp // 8 + 4) % 4)
    )
    k = (INV * kk) % NDEV
    place = jnp.where(r < ROWS, r, ROWS + k * CAP + (r - ROWS) % CAP)
    event = jnp.where(r < ROWS, 0, 1 + k // PER)
    marks = [jnp.where(event == e, 1.0, 0.0) for e in range(EVENTS)]
    mark = jnp.concatenate(marks, axis=0).astype(BF16)
    n = 32 * EVENTS
    ahead = lax.broadcasted_iota(jnp.int32, (128, 128), 0) <= lax.broadcasted_iota(jnp.int32, (128, 128), 1)
    within = jnp.dot(mark, jnp.where(ahead, 1.0, 0.0).astype(BF16), preferred_element_type=F32)
    counts = jnp.dot(mark, jnp.ones((128, 128), BF16), preferred_element_type=F32).astype(BF16)
    before = lax.broadcasted_iota(jnp.int32, (n, n), 1) < lax.broadcasted_iota(jnp.int32, (n, n), 0)
    base = jnp.dot(jnp.where(before, 1.0, 0.0).astype(BF16), counts, preferred_element_type=F32)
    where = base + within - 1.0
    position = jnp.zeros((32, 128), F32)
    for e in range(EVENTS):
        position = position + marks[e] * where[e * 32:(e + 1) * 32]
    order[0:32] = place
    order[64:96] = obs_inst[...]
    order[96:128] = position.astype(jnp.int32)
    acc[...] = jnp.zeros_like(acc)
    major = lax.broadcasted_iota(jnp.int32, (32, 128), 0)
    minor = lax.broadcasted_iota(jnp.int32, (128, 128), 0)
    across = lax.broadcasted_iota(jnp.int32, (1, 128), 1)

    def line(i, _):
        to = order[pl.ds(96 + i, 1), :]
        what = order[pl.ds(i, 1), :]
        high = major == to // 128
        loads = (what // 128, what % 128, jnp.zeros((1, 128), jnp.int32) + i, across, order[pl.ds(64 + i, 1), :])
        a = jnp.concatenate([jnp.where(high, v.astype(F32), 0.0) for v in loads], axis=0).astype(BF16)
        b = jnp.where(minor == to % 128, 1.0, 0.0).astype(BF16)
        acc[...] += lax.dot_general(a, b, (((1,), (1,)), ((), ())), preferred_element_type=F32)
        return 0

    lax.fori_loop(0, 32, line, 0)
    order[0:32] = jnp.clip((acc[0:32] * 128.0 + acc[32:64]).astype(jnp.int32), 0, TABLE - 1)
    order[32:64] = jnp.clip((acc[64:96] * 128.0 + acc[96:128]).astype(jnp.int32), 0, OBS - 1)
    order[64:96] = acc[128:160].astype(jnp.int32)


def weights_kernel(w_in, w_out, obs_src, obs_inst, wi, wo, order, acc, w_send, w_recv):
    x, z, c, y = coords()
    xs, ys, zs, sibling = lines()
    barrier = pltpu.get_barrier_semaphore()
    signal(barrier, ys + xs + zs + sibling)
    pl.semaphore_wait(barrier, 10)

    def send(source, dest, phase, d, dev):
        pltpu.make_async_remote_copy(
            source, dest, w_send, w_recv.at[phase, d - 1], device_id=dev, device_id_type=MESH
        ).start()

    def wait(phase, d, n):
        part = wi.at[d - 1, pl.ds(0, 2 * n)]
        pltpu.make_async_copy(part, part, w_recv.at[phase, d - 1]).wait()

    pieces = (c * 8 + x, c * 8 + 4 + z)
    turns = (1, 3, 2)
    for d in turns:
        for piece in pieces:
            for own, ref in ((w_in, wi), (w_out, wo)):
                send(own.at[piece], ref.at[d - 1, piece], 0, d, ys[d - 1])
    sort(obs_src, obs_inst, order, acc)
    for d in turns:
        wait(0, d, 2)
        for n in range(3):
            for piece, line in zip(pieces, (xs, zs)):
                for ref in (wi, wo):
                    send(ref.at[d - 1, piece], ref.at[d - 1, piece], 1, d, line[n])
    for d in turns:
        wait(1, d, 6)
        for ref in (wi, wo):
            half = ref.at[d - 1, pl.ds(c * 8, 8)]
            send(half, half, 2, d, sibling[0])
    for d in turns:
        wait(2, d, 8)
    for n in (2, 6, 8):
        for ref in (wi, wo):
            part = ref.at[pl.ds(0, 3), pl.ds(0, n)]
            pltpu.make_async_copy(part, part, w_send).wait()


def gather_weights(w_in, w_out, obs_src, obs_inst):
    vmem, any_ = pl.BlockSpec(memory_space=pltpu.VMEM), pl.BlockSpec(memory_space=pl.ANY)
    return pl.pallas_call(
        weights_kernel,
        out_shape=(
            jax.ShapeDtypeStruct((3, 16, 32, D), BF16),
            jax.ShapeDtypeStruct((3, 16, 32, D), BF16),
            jax.ShapeDtypeStruct((128, 128), jnp.int32),
        ),
        in_specs=[vmem] * 4,
        out_specs=(any_, any_, vmem),
        scratch_shapes=[
            pltpu.VMEM((160, 128), F32),
            pltpu.SemaphoreType.DMA,
            pltpu.SemaphoreType.DMA((3, 3)),
        ],
        compiler_params=pltpu.CompilerParams(collective_id=0, has_side_effects=True, vmem_limit_bytes=56 << 20),
        name="gather_weights",
    )(w_in.reshape(16, 32, D), w_out.reshape(16, 32, D), obs_src.reshape(32, 128), obs_inst.reshape(32, 128))


def exchange_kernel(
    latent, gain, lists, order_s, order, w_in, w_out, w_in3, w_out3, feat, embed, w_dec, w_feat, w_head,
    table, decoded,
    wi, wo, send, recv, upd, inner, tab, featb, feats, sfeats, picked, sides, wall, hidden, head, emb, dec,
    load_sem, send_sem, recv_sem, out_sem, s2, s3, s4,
):
    xs, ys, zs, sibling = lines()
    barrier = pltpu.get_barrier_semaphore()
    signal(barrier, ys + zs + xs + sibling)
    own_w = [
        pltpu.make_async_copy(w_in, wi.at[0], load_sem.at[0]),
        pltpu.make_async_copy(w_out, wo.at[0], load_sem.at[1]),
        pltpu.make_async_copy(w_in3, wi.at[pl.ds(1, 3)], load_sem.at[7]),
        pltpu.make_async_copy(w_out3, wo.at[pl.ds(1, 3)], load_sem.at[8]),
    ]
    loads = [
        pltpu.make_async_copy(feat, featb, load_sem.at[2]),
        pltpu.make_async_copy(embed, emb, load_sem.at[3]),
        pltpu.make_async_copy(w_dec, wall.at[pl.ds(0, 512)], load_sem.at[4]),
        pltpu.make_async_copy(w_feat, wall.at[pl.ds(512, 128)], load_sem.at[5]),
        pltpu.make_async_copy(w_head, head, load_sem.at[6]),
    ]
    for load in own_w + loads:
        load.start()

    lane = lax.broadcasted_iota(jnp.int32, (CAP, NDEV), 1)
    cell = lax.broadcasted_iota(jnp.int32, (CAP, ROWS), 1)

    def gather(j, source):
        def hot(i):
            pp, tt = partner(j * PER + i)
            column = jnp.sum(jnp.where(lane == pp * 4 + tt, lists[...], 0).astype(F32), axis=1, keepdims=True)
            return jnp.where(cell == column.astype(jnp.int32), 1.0, 0.0).astype(BF16)

        chosen = jnp.concatenate([hot(i) for i in range(PER)], axis=0)
        rows = jnp.dot(chosen, source[...], preferred_element_type=F32).astype(BF16)
        send[pl.ds(j * PER, PER)] = rows.reshape(PER, CAP, D)

    def put(k):
        pltpu.make_async_remote_copy(
            send.at[k], recv.at[k], send_sem, recv_sem.at[k // PER], device_id=partner(k), device_id_type=MESH
        ).start()

    def start(lo, hi):
        def one(k, _):
            put(k)
            return 0

        lax.fori_loop(lo, hi, one, 0)

    def chunks(lo, hi, source):
        def one(j, _):
            gather(j, source)
            start(j * PER, j * PER + PER)
            return 0

        lax.fori_loop(lo, hi, one, 0)

    def own(i, _):
        at = pl.ds(pl.multiple_of(i * CROWS, CROWS), CROWS)
        upd[at] = process(latent[at], gain[...], wi, wo, inner)
        return 0

    pl.semaphore_wait(barrier, 10)
    signal(s2, zs)
    for load in own_w:
        load.wait()
    own(0, 0)
    pl.semaphore_wait(s2, 3)
    signal(s3, xs)
    own(1, 0)
    pl.semaphore_wait(s3, 3)
    signal(s4, sibling)
    own(2, 0)
    own(3, 0)
    keep = pltpu.make_async_copy(upd, table.at[pl.ds(0, ROWS)], out_sem.at[0])
    keep.start()
    gather(0, upd)
    recv[0] = send[0]
    pl.semaphore_wait(s4, 1)
    start(1, PER)
    chunks(1, CHUNKS, upd)
    for load in loads:
        load.wait()
    load_decoder(emb, wall)
    feats[...] = featb[...].astype(F32)
    pick_sides(order_s, order, feats, sfeats, sides)

    def spread_own(i, _):
        widen(tab, i * CROWS, upd[pl.ds(pl.multiple_of(i * CROWS, CROWS), CROWS)])
        return 0

    lax.fori_loop(0, ROWS // CROWS, spread_own, 0)

    rest = pltpu.make_async_copy(recv, table.at[pl.ds(ROWS, NDEV * CAP)].reshape(NDEV, CAP, D), out_sem.at[2])

    def step(s, _):
        j = s - 1

        @pl.when(j == 0)
        def _():
            pltpu.make_async_copy(recv.at[pl.ds(1, PER - 1)], recv.at[pl.ds(1, PER - 1)], recv_sem.at[0]).wait()

        @pl.when(jnp.logical_and(j > 0, j < CHUNKS))
        def _():
            part = recv.at[pl.ds(j * PER, PER)]
            pltpu.make_async_copy(part, part, recv_sem.at[j]).wait()

        @pl.when(jnp.logical_and(j >= 0, j < CHUNKS))
        def _():
            widen(tab, ROWS + j * CROWS, recv[pl.ds(j * PER, PER)].reshape(CROWS, D))

        @pl.when(s == EVENTS)
        def _():
            rest.start()

        b = (2 * s + 1) // 5

        @pl.when(step_of(b) == s)
        def _():
            at = pl.ds(pl.multiple_of(b * BLOCK, BLOCK), BLOCK)
            dec[at] = decode_block(b, order_s, tab, picked, sides, wall, hidden, head)
            pltpu.make_async_copy(dec.at[at], decoded.at[at], out_sem.at[1]).start()

        return 0

    lax.fori_loop(0, EVENTS + 1, step, 0)
    rest.wait()
    keep.wait()
    pltpu.make_async_copy(dec, decoded, out_sem.at[1]).wait()
    pltpu.make_async_copy(send.at[pl.ds(0, NDEV - 1)], send.at[pl.ds(0, NDEV - 1)], send_sem).wait()


def exchange(latent, gain, send_rows, order, w_in, w_out, w_in3, w_out3, feat, embed, w_dec, w_feat, w_head):
    vmem, any_ = pl.BlockSpec(memory_space=pltpu.VMEM), pl.BlockSpec(memory_space=pl.ANY)
    return pl.pallas_call(
        exchange_kernel,
        out_shape=(
            jax.ShapeDtypeStruct((TABLE, D), BF16),
            jax.ShapeDtypeStruct((OBS, 128), F32),
        ),
        in_specs=[vmem, vmem, vmem, pl.BlockSpec(memory_space=pltpu.SMEM), vmem] + [any_] * 9,
        out_specs=(any_, any_),
        scratch_shapes=[
            pltpu.VMEM((4, 16, 32, D), BF16),
            pltpu.VMEM((4, 16, 32, D), BF16),
            pltpu.VMEM((NDEV, CAP, D), BF16),
            pltpu.VMEM((NDEV, CAP, D), BF16),
            pltpu.VMEM((ROWS, D), BF16),
            pltpu.VMEM((CROWS, FF), BF16),
            pltpu.VMEM((4 * TABLE + 8, 128), F32),
            pltpu.VMEM((OBS, 128), BF16),
            pltpu.VMEM((OBS, 128), F32),
            pltpu.VMEM((OBS, 128), F32),
            pltpu.VMEM((4 * BLOCK + 8, 128), F32),
            pltpu.VMEM((OBS, SIDE), BF16),
            pltpu.VMEM((512 + SIDE, FF), BF16),
            pltpu.VMEM((BLOCK, FF), BF16),
            pltpu.VMEM((FF, 128), BF16),
            pltpu.VMEM((32, FF), F32),
            pltpu.VMEM((OBS, 128), F32),
            pltpu.SemaphoreType.DMA((9,)),
            pltpu.SemaphoreType.DMA,
            pltpu.SemaphoreType.DMA((CHUNKS,)),
            pltpu.SemaphoreType.DMA((3,)),
            pltpu.SemaphoreType.REGULAR,
            pltpu.SemaphoreType.REGULAR,
            pltpu.SemaphoreType.REGULAR,
        ],
        compiler_params=pltpu.CompilerParams(collective_id=1, has_side_effects=True, vmem_limit_bytes=60 << 20),
        name="exchange",
    )(
        latent, gain.reshape(1, D), send_rows.T, order.reshape(-1), order, w_in.reshape(16, 32, D),
        w_out.reshape(16, 32, D), w_in3, w_out3, feat, embed, w_dec, w_feat, w_head,
    )


def finish_kernel(
    order_s, order_v, dec_in, table, feat, embed, w_dec, w_feat, w_head, latent_out, decoded,
    dec, lat, tabb, tab, featb, feats, sfeats, picked, sides, wall, hidden, head, emb, sem, load_sem,
):
    i = pl.program_id(0)
    keep = pltpu.make_async_copy(lat, latent_out, sem.at[2])

    @pl.when(i == 0)
    def _():
        first = pltpu.make_async_copy(table.at[pl.ds(0, ROWS)], lat, sem.at[0])
        second = pltpu.make_async_copy(dec_in, dec, sem.at[1])
        second.start()
        first.start()
        first.wait()
        keep.start()
        second.wait()

        def missed(b):
            last = order_s[b * BLOCK + BLOCK - 1]
            return jnp.where(last < ROWS, 0, 1 + (last - ROWS) // CROWS) > step_of(b)

        any_missed = missed(0)
        for b in range(1, BLOCKS):
            any_missed = jnp.logical_or(any_missed, missed(b))

        @pl.when(any_missed)
        def _():
            loads = [
                pltpu.make_async_copy(feat, featb, load_sem.at[0]),
                pltpu.make_async_copy(embed, emb, load_sem.at[1]),
                pltpu.make_async_copy(w_dec, wall.at[pl.ds(0, 512)], load_sem.at[2]),
                pltpu.make_async_copy(w_feat, wall.at[pl.ds(512, 128)], load_sem.at[3]),
                pltpu.make_async_copy(w_head, head, load_sem.at[4]),
                pltpu.make_async_copy(table, tabb, load_sem.at[5]),
            ]
            for load in loads:
                load.start()
            for load in loads:
                load.wait()
            load_decoder(emb, wall)
            feats[...] = featb[...].astype(F32)
            pick_sides(order_s, order_v, feats, sfeats, sides)

            def spread(n, _):
                widen(tab, n * CROWS, tabb[pl.ds(pl.multiple_of(n * CROWS, CROWS), CROWS)])
                return 0

            lax.fori_loop(0, TABLE // CROWS, spread, 0)

            def again(b, _):
                @pl.when(missed(b))
                def _():
                    dec[pl.ds(pl.multiple_of(b * BLOCK, BLOCK), BLOCK)] = decode_block(
                        b, order_s, tab, picked, sides, wall, hidden, head
                    )

                return 0

            lax.fori_loop(0, BLOCKS, again, 0)

    def back(n, _):
        for u in range(32):
            j = n * 32 + u
            decoded[pl.ds(j, 1), :] = dec[pl.ds(order_s[3 * OBS + i * BLOCK + j], 1), :]
        return 0

    lax.fori_loop(0, BLOCK // 32, back, 0)

    @pl.when(i == BLOCKS - 1)
    def _():
        keep.wait()


def finish(order, dec, table, feat, embed, w_dec, w_feat, w_head):
    any_ = pl.BlockSpec(memory_space=pl.ANY)
    return pl.pallas_call(
        finish_kernel,
        out_shape=(jax.ShapeDtypeStruct((ROWS, D), BF16), jax.ShapeDtypeStruct((OBS, 128), F32)),
        grid_spec=pltpu.PrefetchScalarGridSpec(
            num_scalar_prefetch=1,
            grid=(BLOCKS,),
            in_specs=[pl.BlockSpec((128, 128), lambda i, _: (0, 0))] + [any_] * 7,
            out_specs=(any_, pl.BlockSpec((BLOCK, 128), lambda i, _: (i, 0))),
            scratch_shapes=[
                pltpu.VMEM((OBS, 128), F32),
                pltpu.VMEM((ROWS, D), BF16),
                pltpu.VMEM((TABLE, D), BF16),
                pltpu.VMEM((4 * TABLE + 8, 128), F32),
                pltpu.VMEM((OBS, 128), BF16),
                pltpu.VMEM((OBS, 128), F32),
                pltpu.VMEM((OBS, 128), F32),
                pltpu.VMEM((4 * BLOCK + 8, 128), F32),
                pltpu.VMEM((OBS, SIDE), BF16),
                pltpu.VMEM((512 + SIDE, FF), BF16),
                pltpu.VMEM((BLOCK, FF), BF16),
                pltpu.VMEM((FF, 128), BF16),
                pltpu.VMEM((32, FF), F32),
                pltpu.SemaphoreType.DMA((3,)),
                pltpu.SemaphoreType.DMA((6,)),
            ],
        ),
        compiler_params=pltpu.CompilerParams(vmem_limit_bytes=56 << 20, dimension_semantics=("arbitrary",)),
        name="finish",
    )(order.reshape(-1), order, dec, table, feat, embed, w_dec, w_feat, w_head)


def local(latent, norm_gain, w_in, w_out, send_rows, obs_src, obs_feat, obs_inst, inst_embed, w_dec, w_feat, w_head):
    w_in3, w_out3, order = gather_weights(w_in, w_out, obs_src, obs_inst)
    table, dec = exchange(
        latent, norm_gain, send_rows, order, w_in, w_out, w_in3, w_out3, obs_feat, inst_embed, w_dec, w_feat, w_head
    )
    return finish(order, dec, table, obs_feat, inst_embed, w_dec, w_feat, w_head)


def solution(mesh):
    in_specs = (
        P(("pix", "tp"), None),
        P(),
        P(None, "tp"),
        P("tp", None),
        P(("pix", "tp"), None),
        P(("pix", "tp")),
        P(("pix", "tp"), None),
        P(("pix", "tp")),
        P(),
        P(),
        P(),
        P(),
    )
    out_specs = (P(("pix", "tp"), None), P(("pix", "tp"), None))
    return jax.shard_map(local, mesh=mesh, in_specs=in_specs, out_specs=out_specs, check_vma=False)
```

time: 344 us -> 112 us (0.33); the launches traced: 339 us -> 112 us
  waiting for transfers between devices: 179 us -> 0 us
  Pallas kernels: 0 us -> 111 us
  matrix products: 71.5 us -> 0 us
  local copies, waits for them, and re-layouts: 47 us -> 0 us
  other arithmetic: 16.7 us -> 0 us
  between operations: 14.2 us -> 0.81 us
  starting transfers between devices: 10.6 us -> 0 us
    pallas_call x0 -> x3, Pallas kernels: none -> 111 us  [the longest x1 74.1 us: exchange(): pl.pallas_call(exchange_kernel, out_shape=(jax.ShapeDtypeStruct((TABLE, D...]
    reduce_scatter x1 -> x0, waiting for transfers between devices: 79.7 us -> none  [local(): update = lax.psum_scatter(partials, 'tp', scatter_dimension=0, tiled=True)]
    dot_general x17 -> x0, matrix products: 71.5 us -> none  [the longest x4 29.4 us: decode_block(): pre = pre + jnp.dot(one_hot, inst_embed, precision=lax.Precision.HIGHEST)]
    all_to_all x1 -> x0, waiting for transfers between devices: 50.4 us -> none  [local(): lax.all_to_all(outgoing, ('pix', 'tp'), split_axis=0, concat_axis=0, tile...]
    all_gather x1 -> x0, waiting for transfers between devices: 48.8 us -> none  [local(): lax.all_gather(normed, 'tp', axis=0, tiled=True)]
    gather x5 -> x0, local copies, waits for them, and re-layouts: 45.9 us -> none  [the longest x4 28.6 us: decode_block(): gathered = jnp.take(table, sources, axis=0)]
    all_to_all x1 -> x0, starting transfers between devices: 10.5 us -> none  [local(): lax.all_to_all(outgoing, ('pix', 'tp'), split_axis=0, concat_axis=0, tile...]
    concatenate x1 -> x0, other arithmetic: 4.92 us -> none  [local(): table = jnp.concatenate([updated, arrived], axis=0)]
  transfers between devices with their start and end apart: 3 -> 0, of which waited for: 3 -> 0; matrix products, arithmetic and copies ran while one was open for 0% -> 0% of each run, Pallas kernels for 0% -> 0%
where the time goes in v2:
time: 112 us
  Pallas kernels  111 us (99%)
    pallas_call x1, Pallas kernels, exchange(): pl.pallas_call(exchange_kernel, out_shape=(jax.ShapeDtypeStruct((TABLE, D...  74.1 us
    pallas_call x1, Pallas kernels, gather_weights(): pl.pallas_call(weights_kernel, out_shape=(jax.ShapeDtypeStruct((3, 16, 32...  26 us
    pallas_call x1, Pallas kernels, finish(): pl.pallas_call(finish_kernel, out_shape=(jax.ShapeDtypeStruct((ROWS, D),...  10.7 us

profile of v2, /device:TPU:27, one launch (start us, length us, event | category | flops | bytes accessed | tf_op | source)
XLA Modules:
  0.0 111.6 jit_solution(16492596175604987836)
XLA Ops:
  0.6 26.0 %gather_weights.1 = (bf16[3,16,32,512]{3,2,1,0:T(8,128)(2,1)}, bf16[3,16,32,512]{3,2,1,0:T(8,128)(2,1)}, s32[128,128]{1,0:T(8,128)}) custom-call(bf16[16,32,512]{2,1,0:T(8,128)(2,1)} %bitcast.7, bf16[16,32,512]{2,1,0:T(8,128)(2,1)} %bitcast.9, s32[32,128]{1,0:T(8,128)} %bitcast.13, s32[32,128]{1,0:T(8,128)} %bitcast.14), custom_call_target="tpu_custom_call" | custom-call | tf_op jit(solution)/shard_map/gather_weights/pallas_call | solution.py:222
  26.6 74.1 %exchange.1 = (bf16[5120,512]{1,0:T(8,128)(2,1)}, f32[4096,128]{1,0:T(8,128)}) custom-call(bf16[1024,512]{1,0:T(8,128)(2,1)} %latent.1, f32[1,512]{1,0:T(1,128)} %bitcast.16, s32[32,128]{1,0:T(8,128)} %bitcast.15, s32[16384]{0:T(1024)} %bitcast.11, s32[128,128]{1,0:T(8,128)} %get-tuple-element.7.order.order_v, bf16[16,32,512]{2,1,0:T(8,128)(2,1)} %bitcast.8, ...), custom_call_target="tpu_custom_call" | custom-call | tf_op jit(solution)/shard_map/exchange/pallas_call | solution.py:376
  100.7 10.7 %finish.1 = (bf16[1024,512]{1,0:T(8,128)(2,1)}, f32[4096,128]{1,0:T(8,128)}) custom-call(s32[16384]{0:T(1024)} %bitcast.12, s32[128,128]{1,0:T(8,128)} %get-tuple-element.7.order.order_v, f32[4096,128]{1,0:T(8,128)} %get-tuple-element.10.dec_in, bf16[5120,512]{1,0:T(8,128)(2,1)} %get-tuple-element.11.table, bf16[4096,128]{1,0:T(8,128)(2,1)} %feat.3, ...), custom_call_target="tpu_custom_call" | custom-call | tf_op jit(solution)/shard_map/finish/pallas_call | solution.py:493

commit v3 on v2

--- a/solution.py
+++ b/solution.py
@@ -22,6 +22,7 @@
 BLOCK = 512
 BLOCKS = OBS // BLOCK
 EVENTS = CHUNKS + 1
+OUT = 1024
 SIDE = 192
 
 
@@ -47,17 +48,11 @@
     return (5 * block) // 2
 
 
-def process(rows, gain, wi, wo, inner):
+def normalise(rows, gain):
     values = rows.astype(F32)
     center = values - jnp.mean(values, axis=-1, keepdims=True)
     spread = jnp.mean(center * center, axis=-1, keepdims=True)
-    normed = (center * lax.rsqrt(spread + 1e-05) * gain).astype(BF16)
-    for d in range(4):
-        inner[:, d * D:(d + 1) * D] = gelu(
-            jnp.dot(normed, wi[d].reshape(D, D), preferred_element_type=F32)
-        ).astype(BF16)
-    update = jnp.dot(inner[...], wo[...].reshape(FF, D), preferred_element_type=F32)
-    return (values + update).astype(BF16)
+    return (center * lax.rsqrt(spread + 1e-05) * gain).astype(BF16)
 
 
 def widen(tab, start, rows):
@@ -114,10 +109,11 @@
 
 def lines():
     x, z, c, y = coords()
+    ys = [(x * 8 + z * 2 + c, (y + 4 - d) % 4) for d in (1, 2, 3)]
+    zs = [(x * 8 + ((z + d) % 4) * 2 + c, y) for d in (1, 2, 3)]
     xs = [(((x + d) % 4) * 8 + z * 2 + c, y) for d in (1, 2, 3)]
-    zs = [(x * 8 + ((z + d) % 4) * 2 + c, y) for d in (1, 2, 3)]
-    ys = [(x * 8 + z * 2 + c, (y + 4 - d) % 4) for d in (1, 2, 3)]
-    return xs, ys, zs, [(x * 8 + z * 2 + 1 - c, y)]
+    others = [(((x + d) % 4) * 8 + z * 2 + 1 - c, y) for d in (0, 1, 2, 3)]
+    return ys, zs, xs, others
 
 
 def signal(sem, who):
@@ -125,7 +121,7 @@
         pl.semaphore_signal(sem, inc=1, device_id=dev, device_id_type=MESH)
 
 
-def sort(obs_src, obs_inst, order, acc):
+def sort(obs_src, obs_inst, order, place, acc):
     x, z, c, y = coords()
     r = obs_src[...]
     s = jnp.maximum(r - ROWS, 0) // CAP
@@ -137,7 +133,7 @@
         + 32 * ((x - sp // 8 + 4) % 4)
     )
     k = (INV * kk) % NDEV
-    place = jnp.where(r < ROWS, r, ROWS + k * CAP + (r - ROWS) % CAP)
+    row = jnp.where(r < ROWS, r, ROWS + k * CAP + (r - ROWS) % CAP)
     event = jnp.where(r < ROWS, 0, 1 + k // PER)
     marks = [jnp.where(event == e, 1.0, 0.0) for e in range(EVENTS)]
     mark = jnp.concatenate(marks, axis=0).astype(BF16)
@@ -151,16 +147,16 @@
     position = jnp.zeros((32, 128), F32)
     for e in range(EVENTS):
         position = position + marks[e] * where[e * 32:(e + 1) * 32]
-    order[0:32] = place
+    order[0:32] = row
     order[64:96] = obs_inst[...]
-    order[96:128] = position.astype(jnp.int32)
+    place[0:32] = position.astype(jnp.int32)
     acc[...] = jnp.zeros_like(acc)
     major = lax.broadcasted_iota(jnp.int32, (32, 128), 0)
     minor = lax.broadcasted_iota(jnp.int32, (128, 128), 0)
     across = lax.broadcasted_iota(jnp.int32, (1, 128), 1)
 
     def line(i, _):
-        to = order[pl.ds(96 + i, 1), :]
+        to = place[pl.ds(i, 1), :]
         what = order[pl.ds(i, 1), :]
         high = major == to // 128
         loads = (what // 128, what % 128, jnp.zeros((1, 128), jnp.int32) + i, across, order[pl.ds(64 + i, 1), :])
@@ -173,13 +169,27 @@
     order[0:32] = jnp.clip((acc[0:32] * 128.0 + acc[32:64]).astype(jnp.int32), 0, TABLE - 1)
     order[32:64] = jnp.clip((acc[64:96] * 128.0 + acc[96:128]).astype(jnp.int32), 0, OBS - 1)
     order[64:96] = acc[128:160].astype(jnp.int32)
-
-
-def weights_kernel(w_in, w_out, obs_src, obs_inst, wi, wo, order, acc, w_send, w_recv):
+    for b in range(BLOCKS):
+        last = (b + 1) * (BLOCK // 128) - 1
+        place[32 + b:33 + b] = order[last:last + 1]
+
+
+def process_kernel(
+    latent, gain, w_in, w_out, obs_src, obs_inst, upd, order, place,
+    wi, wo, normed, total, acc, w_send, w_recv,
+):
     x, z, c, y = coords()
-    xs, ys, zs, sibling = lines()
+    ys, zs, xs, others = lines()
     barrier = pltpu.get_barrier_semaphore()
-    signal(barrier, ys + xs + zs + sibling)
+    signal(barrier, ys + xs + zs + others[:1])
+
+    def prepare(i, _):
+        at = pl.ds(pl.multiple_of(i * 256, 256), 256)
+        normed[at] = normalise(latent[at], gain[...])
+        total[at] = latent[at].astype(F32)
+        return 0
+
+    lax.fori_loop(0, ROWS // 256, prepare, 0)
     pl.semaphore_wait(barrier, 10)
 
     def send(source, dest, phase, d, dev):
@@ -190,6 +200,15 @@
     def wait(phase, d, n):
         part = wi.at[d - 1, pl.ds(0, 2 * n)]
         pltpu.make_async_copy(part, part, w_recv.at[phase, d - 1]).wait()
+
+    def shard(first, second):
+        def rows(i, _):
+            at = pl.ds(pl.multiple_of(i * 512, 512), 512)
+            inner = gelu(jnp.dot(normed[at], first, preferred_element_type=F32)).astype(BF16)
+            total[at] += jnp.dot(inner, second, preferred_element_type=F32)
+            return 0
+
+        lax.fori_loop(0, ROWS // 512, rows, 0)
 
     pieces = (c * 8 + x, c * 8 + 4 + z)
     turns = (1, 3, 2)
@@ -197,70 +216,74 @@
         for piece in pieces:
             for own, ref in ((w_in, wi), (w_out, wo)):
                 send(own.at[piece], ref.at[d - 1, piece], 0, d, ys[d - 1])
-    sort(obs_src, obs_inst, order, acc)
+    shard(w_in[...].reshape(D, D), w_out[...].reshape(D, D))
     for d in turns:
         wait(0, d, 2)
         for n in range(3):
             for piece, line in zip(pieces, (xs, zs)):
                 for ref in (wi, wo):
                     send(ref.at[d - 1, piece], ref.at[d - 1, piece], 1, d, line[n])
+    sort(obs_src, obs_inst, order, place, acc)
     for d in turns:
         wait(1, d, 6)
         for ref in (wi, wo):
             half = ref.at[d - 1, pl.ds(c * 8, 8)]
-            send(half, half, 2, d, sibling[0])
+            send(half, half, 2, d, others[0])
     for d in turns:
         wait(2, d, 8)
+        shard(wi[d - 1].reshape(D, D), wo[d - 1].reshape(D, D))
+
+    upd[...] = total[...].astype(BF16)
     for n in (2, 6, 8):
         for ref in (wi, wo):
             part = ref.at[pl.ds(0, 3), pl.ds(0, n)]
             pltpu.make_async_copy(part, part, w_send).wait()
 
 
-def gather_weights(w_in, w_out, obs_src, obs_inst):
-    vmem, any_ = pl.BlockSpec(memory_space=pltpu.VMEM), pl.BlockSpec(memory_space=pl.ANY)
+def process(latent, gain, w_in, w_out, obs_src, obs_inst):
+    vmem = pl.BlockSpec(memory_space=pltpu.VMEM)
     return pl.pallas_call(
-        weights_kernel,
+        process_kernel,
         out_shape=(
-            jax.ShapeDtypeStruct((3, 16, 32, D), BF16),
-            jax.ShapeDtypeStruct((3, 16, 32, D), BF16),
-            jax.ShapeDtypeStruct((128, 128), jnp.int32),
+            jax.ShapeDtypeStruct((ROWS, D), BF16),
+            jax.ShapeDtypeStruct((96, 128), jnp.int32),
+            jax.ShapeDtypeStruct((32 + BLOCKS, 128), jnp.int32),
         ),
-        in_specs=[vmem] * 4,
-        out_specs=(any_, any_, vmem),
+        in_specs=[vmem] * 6,
+        out_specs=(vmem,) * 3,
         scratch_shapes=[
+            pltpu.VMEM((3, 16, 32, D), BF16),
+            pltpu.VMEM((3, 16, 32, D), BF16),
+            pltpu.VMEM((ROWS, D), BF16),
+            pltpu.VMEM((ROWS, D), F32),
             pltpu.VMEM((160, 128), F32),
             pltpu.SemaphoreType.DMA,
             pltpu.SemaphoreType.DMA((3, 3)),
         ],
         compiler_params=pltpu.CompilerParams(collective_id=0, has_side_effects=True, vmem_limit_bytes=56 << 20),
-        name="gather_weights",
-    )(w_in.reshape(16, 32, D), w_out.reshape(16, 32, D), obs_src.reshape(32, 128), obs_inst.reshape(32, 128))
+        name="process",
+    )(
+        latent, gain.reshape(1, D), w_in.reshape(16, 32, D), w_out.reshape(16, 32, D),
+        obs_src.reshape(32, 128), obs_inst.reshape(32, 128),
+    )
 
 
 def exchange_kernel(
-    latent, gain, lists, order_s, order, w_in, w_out, w_in3, w_out3, feat, embed, w_dec, w_feat, w_head,
-    table, decoded,
-    wi, wo, send, recv, upd, inner, tab, featb, feats, sfeats, picked, sides, wall, hidden, head, emb, dec,
-    load_sem, send_sem, recv_sem, out_sem, s2, s3, s4,
+    upd, lists, order_s, order, feat, embed, w_dec, w_feat, w_head, table, decoded,
+    send, recv, tab, featb, feats, sfeats, picked, sides, wall, hidden, head, emb, dec,
+    load_sem, send_sem, recv_sem, out_sem, s2, s3,
 ):
-    xs, ys, zs, sibling = lines()
+    ys, zs, xs, others = lines()
     barrier = pltpu.get_barrier_semaphore()
-    signal(barrier, ys + zs + xs + sibling)
-    own_w = [
-        pltpu.make_async_copy(w_in, wi.at[0], load_sem.at[0]),
-        pltpu.make_async_copy(w_out, wo.at[0], load_sem.at[1]),
-        pltpu.make_async_copy(w_in3, wi.at[pl.ds(1, 3)], load_sem.at[7]),
-        pltpu.make_async_copy(w_out3, wo.at[pl.ds(1, 3)], load_sem.at[8]),
+    signal(barrier, ys + zs + xs + others)
+    loads = [
+        pltpu.make_async_copy(feat, featb, load_sem.at[0]),
+        pltpu.make_async_copy(embed, emb, load_sem.at[1]),
+        pltpu.make_async_copy(w_dec, wall.at[pl.ds(0, 512)], load_sem.at[2]),
+        pltpu.make_async_copy(w_feat, wall.at[pl.ds(512, 128)], load_sem.at[3]),
+        pltpu.make_async_copy(w_head, head, load_sem.at[4]),
     ]
-    loads = [
-        pltpu.make_async_copy(feat, featb, load_sem.at[2]),
-        pltpu.make_async_copy(embed, emb, load_sem.at[3]),
-        pltpu.make_async_copy(w_dec, wall.at[pl.ds(0, 512)], load_sem.at[4]),
-        pltpu.make_async_copy(w_feat, wall.at[pl.ds(512, 128)], load_sem.at[5]),
-        pltpu.make_async_copy(w_head, head, load_sem.at[6]),
-    ]
-    for load in own_w + loads:
+    for load in loads:
         load.start()
 
     lane = lax.broadcasted_iota(jnp.int32, (CAP, NDEV), 1)
@@ -296,30 +319,17 @@
 
         lax.fori_loop(lo, hi, one, 0)
 
-    def own(i, _):
-        at = pl.ds(pl.multiple_of(i * CROWS, CROWS), CROWS)
-        upd[at] = process(latent[at], gain[...], wi, wo, inner)
-        return 0
-
-    pl.semaphore_wait(barrier, 10)
-    signal(s2, zs)
-    for load in own_w:
-        load.wait()
-    own(0, 0)
-    pl.semaphore_wait(s2, 3)
-    signal(s3, xs)
-    own(1, 0)
-    pl.semaphore_wait(s3, 3)
-    signal(s4, sibling)
-    own(2, 0)
-    own(3, 0)
-    keep = pltpu.make_async_copy(upd, table.at[pl.ds(0, ROWS)], out_sem.at[0])
-    keep.start()
     gather(0, upd)
     recv[0] = send[0]
-    pl.semaphore_wait(s4, 1)
-    start(1, PER)
-    chunks(1, CHUNKS, upd)
+    pl.semaphore_wait(barrier, 13)
+    signal(s2, zs)
+    gather(1, upd)
+    pl.semaphore_wait(s2, 3)
+    signal(s3, xs + others)
+    gather(2, upd)
+    pl.semaphore_wait(s3, 7)
+    start(1, 3 * PER)
+    chunks(3, CHUNKS, upd)
     for load in loads:
         load.wait()
     load_decoder(emb, wall)
@@ -332,7 +342,7 @@
 
     lax.fori_loop(0, ROWS // CROWS, spread_own, 0)
 
-    rest = pltpu.make_async_copy(recv, table.at[pl.ds(ROWS, NDEV * CAP)].reshape(NDEV, CAP, D), out_sem.at[2])
+    rest = pltpu.make_async_copy(recv, table, out_sem.at[0])
 
     def step(s, _):
         j = s - 1
@@ -366,28 +376,23 @@
 
     lax.fori_loop(0, EVENTS + 1, step, 0)
     rest.wait()
-    keep.wait()
     pltpu.make_async_copy(dec, decoded, out_sem.at[1]).wait()
     pltpu.make_async_copy(send.at[pl.ds(0, NDEV - 1)], send.at[pl.ds(0, NDEV - 1)], send_sem).wait()
 
 
-def exchange(latent, gain, send_rows, order, w_in, w_out, w_in3, w_out3, feat, embed, w_dec, w_feat, w_head):
+def exchange(upd, send_rows, order, feat, embed, w_dec, w_feat, w_head):
     vmem, any_ = pl.BlockSpec(memory_space=pltpu.VMEM), pl.BlockSpec(memory_space=pl.ANY)
     return pl.pallas_call(
         exchange_kernel,
         out_shape=(
-            jax.ShapeDtypeStruct((TABLE, D), BF16),
+            jax.ShapeDtypeStruct((NDEV, CAP, D), BF16),
             jax.ShapeDtypeStruct((OBS, 128), F32),
         ),
-        in_specs=[vmem, vmem, vmem, pl.BlockSpec(memory_space=pltpu.SMEM), vmem] + [any_] * 9,
+        in_specs=[vmem, vmem, pl.BlockSpec(memory_space=pltpu.SMEM), vmem] + [any_] * 5,
         out_specs=(any_, any_),
         scratch_shapes=[
-            pltpu.VMEM((4, 16, 32, D), BF16),
-            pltpu.VMEM((4, 16, 32, D), BF16),
             pltpu.VMEM((NDEV, CAP, D), BF16),
             pltpu.VMEM((NDEV, CAP, D), BF16),
-            pltpu.VMEM((ROWS, D), BF16),
-            pltpu.VMEM((CROWS, FF), BF16),
             pltpu.VMEM((4 * TABLE + 8, 128), F32),
             pltpu.VMEM((OBS, 128), BF16),
             pltpu.VMEM((OBS, 128), F32),
@@ -399,32 +404,28 @@
             pltpu.VMEM((FF, 128), BF16),
             pltpu.VMEM((32, FF), F32),
             pltpu.VMEM((OBS, 128), F32),
-            pltpu.SemaphoreType.DMA((9,)),
+            pltpu.SemaphoreType.DMA((5,)),
             pltpu.SemaphoreType.DMA,
             pltpu.SemaphoreType.DMA((CHUNKS,)),
-            pltpu.SemaphoreType.DMA((3,)),
-            pltpu.SemaphoreType.REGULAR,
+            pltpu.SemaphoreType.DMA((2,)),
             pltpu.SemaphoreType.REGULAR,
             pltpu.SemaphoreType.REGULAR,
         ],
         compiler_params=pltpu.CompilerParams(collective_id=1, has_side_effects=True, vmem_limit_bytes=60 << 20),
         name="exchange",
-    )(
-        latent, gain.reshape(1, D), send_rows.T, order.reshape(-1), order, w_in.reshape(16, 32, D),
-        w_out.reshape(16, 32, D), w_in3, w_out3, feat, embed, w_dec, w_feat, w_head,
-    )
+    )(upd, send_rows.T, order.reshape(-1), order, feat, embed, w_dec, w_feat, w_head)
 
 
 def finish_kernel(
-    order_s, order_v, dec_in, table, feat, embed, w_dec, w_feat, w_head, latent_out, decoded,
-    dec, lat, tabb, tab, featb, feats, sfeats, picked, sides, wall, hidden, head, emb, sem, load_sem,
+    place, order, upd, dec_in, table, feat, embed, w_dec, w_feat, w_head, latent_out, decoded,
+    dec, lat, tabb, tab, featb, feats, sfeats, picked, sides, wall, hidden, head, emb, order_s, order_v, sem, load_sem,
 ):
     i = pl.program_id(0)
     keep = pltpu.make_async_copy(lat, latent_out, sem.at[2])
 
     @pl.when(i == 0)
     def _():
-        first = pltpu.make_async_copy(table.at[pl.ds(0, ROWS)], lat, sem.at[0])
+        first = pltpu.make_async_copy(upd, lat, sem.at[0])
         second = pltpu.make_async_copy(dec_in, dec, sem.at[1])
         second.start()
         first.start()
@@ -433,7 +434,7 @@
         second.wait()
 
         def missed(b):
-            last = order_s[b * BLOCK + BLOCK - 1]
+            last = place[(32 + b) * 128 + 127]
             return jnp.where(last < ROWS, 0, 1 + (last - ROWS) // CROWS) > step_of(b)
 
         any_missed = missed(0)
@@ -449,6 +450,7 @@
                 pltpu.make_async_copy(w_feat, wall.at[pl.ds(512, 128)], load_sem.at[3]),
                 pltpu.make_async_copy(w_head, head, load_sem.at[4]),
                 pltpu.make_async_copy(table, tabb, load_sem.at[5]),
+                pltpu.make_async_copy(order, order_v, load_sem.at[6]),
             ]
             for load in loads:
                 load.start()
@@ -456,13 +458,28 @@
                 load.wait()
             load_decoder(emb, wall)
             feats[...] = featb[...].astype(F32)
+
+            def to_scalar(n, _):
+                to = order_s.at[pl.ds(pl.multiple_of(n * 128, 128), 128)]
+                copy = pltpu.make_async_copy(order_v.at[n], to, load_sem.at[7])
+                copy.start()
+                copy.wait()
+                return 0
+
+            lax.fori_loop(0, 64, to_scalar, 0)
             pick_sides(order_s, order_v, feats, sfeats, sides)
 
+            def spread_own(n, _):
+                widen(tab, n * CROWS, lat[pl.ds(pl.multiple_of(n * CROWS, CROWS), CROWS)])
+                return 0
+
+            lax.fori_loop(0, ROWS // CROWS, spread_own, 0)
+
             def spread(n, _):
-                widen(tab, n * CROWS, tabb[pl.ds(pl.multiple_of(n * CROWS, CROWS), CROWS)])
+                widen(tab, ROWS + n * CROWS, tabb[pl.ds(n * PER, PER)].reshape(CROWS, D))
                 return 0
 
-            lax.fori_loop(0, TABLE // CROWS, spread, 0)
+            lax.fori_loop(0, CHUNKS, spread, 0)
 
             def again(b, _):
                 @pl.when(missed(b))
@@ -478,30 +495,30 @@
     def back(n, _):
         for u in range(32):
             j = n * 32 + u
-            decoded[pl.ds(j, 1), :] = dec[pl.ds(order_s[3 * OBS + i * BLOCK + j], 1), :]
-        return 0
-
-    lax.fori_loop(0, BLOCK // 32, back, 0)
-
-    @pl.when(i == BLOCKS - 1)
+            decoded[pl.ds(j, 1), :] = dec[pl.ds(place[i * OUT + j], 1), :]
+        return 0
+
+    lax.fori_loop(0, OUT // 32, back, 0)
+
+    @pl.when(i == OBS // OUT - 1)
     def _():
         keep.wait()
 
 
-def finish(order, dec, table, feat, embed, w_dec, w_feat, w_head):
+def finish(place, order, upd, dec, table, feat, embed, w_dec, w_feat, w_head):
     any_ = pl.BlockSpec(memory_space=pl.ANY)
     return pl.pallas_call(
         finish_kernel,
         out_shape=(jax.ShapeDtypeStruct((ROWS, D), BF16), jax.ShapeDtypeStruct((OBS, 128), F32)),
         grid_spec=pltpu.PrefetchScalarGridSpec(
             num_scalar_prefetch=1,
-            grid=(BLOCKS,),
-            in_specs=[pl.BlockSpec((128, 128), lambda i, _: (0, 0))] + [any_] * 7,
-            out_specs=(any_, pl.BlockSpec((BLOCK, 128), lambda i, _: (i, 0))),
+            grid=(OBS // OUT,),
+            in_specs=[any_] * 9,
+            out_specs=(any_, pl.BlockSpec((OUT, 128), lambda i, _: (i, 0))),
             scratch_shapes=[
                 pltpu.VMEM((OBS, 128), F32),
                 pltpu.VMEM((ROWS, D), BF16),
-                pltpu.VMEM((TABLE, D), BF16),
+                pltpu.VMEM((NDEV, CAP, D), BF16),
                 pltpu.VMEM((4 * TABLE + 8, 128), F32),
                 pltpu.VMEM((OBS, 128), BF16),
                 pltpu.VMEM((OBS, 128), F32),
@@ -512,21 +529,21 @@
                 pltpu.VMEM((BLOCK, FF), BF16),
                 pltpu.VMEM((FF, 128), BF16),
                 pltpu.VMEM((32, FF), F32),
+                pltpu.SMEM((2 * OBS,), jnp.int32),
+                pltpu.VMEM((96, 128), jnp.int32),
                 pltpu.SemaphoreType.DMA((3,)),
-                pltpu.SemaphoreType.DMA((6,)),
+                pltpu.SemaphoreType.DMA((8,)),
             ],
         ),
         compiler_params=pltpu.CompilerParams(vmem_limit_bytes=56 << 20, dimension_semantics=("arbitrary",)),
         name="finish",
-    )(order.reshape(-1), order, dec, table, feat, embed, w_dec, w_feat, w_head)
+    )(place.reshape(-1), order, upd, dec, table, feat, embed, w_dec, w_feat, w_head)
 
 
 def local(latent, norm_gain, w_in, w_out, send_rows, obs_src, obs_feat, obs_inst, inst_embed, w_dec, w_feat, w_head):
-    w_in3, w_out3, order = gather_weights(w_in, w_out, obs_src, obs_inst)
-    table, dec = exchange(
-        latent, norm_gain, send_rows, order, w_in, w_out, w_in3, w_out3, obs_feat, inst_embed, w_dec, w_feat, w_head
-    )
-    return finish(order, dec, table, obs_feat, inst_embed, w_dec, w_feat, w_head)
+    upd, order, place = process(latent, norm_gain, w_in, w_out, obs_src, obs_inst)
+    table, dec = exchange(upd, send_rows, order, obs_feat, inst_embed, w_dec, w_feat, w_head)
+    return finish(place, order, upd, dec, table, obs_feat, inst_embed, w_dec, w_feat, w_head)
 
 
 def solution(mesh):

time: 112 us -> 105 us (0.938)
  the two profiles are of different devices: /device:TPU:27 before, /device:TPU:1 now
where the time goes in v3:
time: 105 us
  Pallas kernels  104 us (99%)
    pallas_call x1, Pallas kernels, exchange(): pl.pallas_call(exchange_kernel, out_shape=(jax.ShapeDtypeStruct((NDEV, CA...  64.5 us
    pallas_call x1, Pallas kernels, process(): pl.pallas_call(process_kernel, out_shape=(jax.ShapeDtypeStruct((ROWS, D),...  30.7 us
    pallas_call x1, Pallas kernels, finish(): pl.pallas_call(finish_kernel, out_shape=(jax.ShapeDtypeStruct((ROWS, D),...  8.87 us

profile of v3, /device:TPU:1, one launch (start us, length us, event | category | flops | bytes accessed | tf_op | source)
XLA Modules:
  0.0 104.7 jit_solution(16181188082841774095)
XLA Ops:
  0.6 30.7 %process.1 = (bf16[1024,512]{1,0:T(8,128)(2,1)}, s32[96,128]{1,0:T(8,128)}, s32[40,128]{1,0:T(8,128)}) custom-call(bf16[1024,512]{1,0:T(8,128)(2,1)} %latent.1, f32[1,512]{1,0:T(1,128)} %bitcast.15, bf16[16,32,512]{2,1,0:T(8,128)(2,1)} %bitcast.8, bf16[16,32,512]{2,1,0:T(8,128)(2,1)} %bitcast.9, s32[32,128]{1,0:T(8,128)} %bitcast.12, s32[32,128]{1,0:T(8,128)} %bitcast.13), custom_call_target="tpu_custom_call" | custom-call | tf_op jit(solution)/shard_map/process/pallas_call | solution.py:245
  31.4 64.5 %exchange.1 = (bf16[128,32,512]{2,1,0:T(8,128)(2,1)}, f32[4096,128]{1,0:T(8,128)}) custom-call(bf16[1024,512]{1,0:T(8,128)(2,1)} %get-tuple-element.9.upd, s32[32,128]{1,0:T(8,128)} %bitcast.14, s32[12288]{0:T(1024)} %bitcast.10, s32[96,128]{1,0:T(8,128)} %get-tuple-element.8.order, bf16[4096,128]{1,0:T(8,128)(2,1)} %feat.3, f32[32,2048]{1,0:T(8,128)} %embed.3, ...), custom_call_target="tpu_custom_call" | custom-call | tf_op jit(solution)/shard_map/exchange/pallas_call | solution.py:385
  95.8 8.9 %finish.1 = (bf16[1024,512]{1,0:T(8,128)(2,1)}, f32[4096,128]{1,0:T(8,128)}) custom-call(s32[5120]{0:T(1024)} %bitcast.11, s32[96,128]{1,0:T(8,128)} %get-tuple-element.8.order, bf16[1024,512]{1,0:T(8,128)(2,1)} %get-tuple-element.9.upd, f32[4096,128]{1,0:T(8,128)} %get-tuple-element.10.dec_in, bf16[128,32,512]{2,1,0:T(8,128)(2,1)} %get-tuple-element.11.table, ...), custom_call_target="tpu_custom_call" | custom-call | tf_op jit(solution)/shard_map/finish/pallas_call | solution.py:510

commit v4 on v3

--- a/solution.py
+++ b/solution.py
@@ -22,7 +22,8 @@
 BLOCK = 512
 BLOCKS = OBS // BLOCK
 EVENTS = CHUNKS + 1
-OUT = 1024
+EARLY = 6
+LATE = OBS - EARLY * BLOCK
 SIDE = 192
 
 
@@ -45,7 +46,7 @@
 
 
 def step_of(block):
-    return (5 * block) // 2
+    return (5 * block) // 2 - block // 6 + block // 7
 
 
 def normalise(rows, gain):
@@ -172,16 +173,24 @@
     for b in range(BLOCKS):
         last = (b + 1) * (BLOCK // 128) - 1
         place[32 + b:33 + b] = order[last:last + 1]
+    place[40:48] = order[32 + EARLY * (BLOCK // 128):64]
 
 
 def process_kernel(
-    latent, gain, w_in, w_out, obs_src, obs_inst, upd, order, place,
-    wi, wo, normed, total, acc, w_send, w_recv,
+    latent_h, gain, w_in_h, w_out_h, obs_src, obs_inst, upd, order, place,
+    latent, w_in, w_out, wi, wo, normed, total, acc, load_sem, w_send, w_recv,
 ):
     x, z, c, y = coords()
     ys, zs, xs, others = lines()
     barrier = pltpu.get_barrier_semaphore()
+    loads = [
+        pltpu.make_async_copy(source, ref, load_sem.at[n])
+        for n, (source, ref) in enumerate(((latent_h, latent), (w_in_h, w_in), (w_out_h, w_out)))
+    ]
+    for load in loads:
+        load.start()
     signal(barrier, ys + xs + zs + others[:1])
+    loads[0].wait()
 
     def prepare(i, _):
         at = pl.ds(pl.multiple_of(i * 256, 256), 256)
@@ -190,6 +199,8 @@
         return 0
 
     lax.fori_loop(0, ROWS // 256, prepare, 0)
+    for load in loads[1:]:
+        load.wait()
     pl.semaphore_wait(barrier, 10)
 
     def send(source, dest, phase, d, dev):
@@ -241,22 +252,26 @@
 
 
 def process(latent, gain, w_in, w_out, obs_src, obs_inst):
-    vmem = pl.BlockSpec(memory_space=pltpu.VMEM)
+    vmem, any_ = pl.BlockSpec(memory_space=pltpu.VMEM), pl.BlockSpec(memory_space=pl.ANY)
     return pl.pallas_call(
         process_kernel,
         out_shape=(
             jax.ShapeDtypeStruct((ROWS, D), BF16),
             jax.ShapeDtypeStruct((96, 128), jnp.int32),
-            jax.ShapeDtypeStruct((32 + BLOCKS, 128), jnp.int32),
+            jax.ShapeDtypeStruct((48, 128), jnp.int32),
         ),
-        in_specs=[vmem] * 6,
+        in_specs=[any_, vmem, any_, any_, vmem, vmem],
         out_specs=(vmem,) * 3,
         scratch_shapes=[
+            pltpu.VMEM((ROWS, D), BF16),
+            pltpu.VMEM((16, 32, D), BF16),
+            pltpu.VMEM((16, 32, D), BF16),
             pltpu.VMEM((3, 16, 32, D), BF16),
             pltpu.VMEM((3, 16, 32, D), BF16),
             pltpu.VMEM((ROWS, D), BF16),
             pltpu.VMEM((ROWS, D), F32),
             pltpu.VMEM((160, 128), F32),
+            pltpu.SemaphoreType.DMA((3,)),
             pltpu.SemaphoreType.DMA,
             pltpu.SemaphoreType.DMA((3, 3)),
         ],
@@ -269,8 +284,9 @@
 
 
 def exchange_kernel(
-    upd, lists, order_s, order, feat, embed, w_dec, w_feat, w_head, table, decoded,
-    send, recv, tab, featb, feats, sfeats, picked, sides, wall, hidden, head, emb, dec,
+    upd_h, lists, order_h, order_vh, place_h, feat, embed, w_dec, w_feat, w_head, table, natural, late,
+    upd, order_s, order, place_s,
+    send, recv, tab, featb, feats, sfeats, picked, sides, wall, hidden, head, emb, dec, nat,
     load_sem, send_sem, recv_sem, out_sem, s2, s3,
 ):
     ys, zs, xs, others = lines()
@@ -282,7 +298,12 @@
         pltpu.make_async_copy(w_dec, wall.at[pl.ds(0, 512)], load_sem.at[2]),
         pltpu.make_async_copy(w_feat, wall.at[pl.ds(512, 128)], load_sem.at[3]),
         pltpu.make_async_copy(w_head, head, load_sem.at[4]),
+        pltpu.make_async_copy(order_h, order_s, load_sem.at[5]),
+        pltpu.make_async_copy(order_vh, order, load_sem.at[6]),
+        pltpu.make_async_copy(place_h, place_s, load_sem.at[7]),
     ]
+    rows_in = pltpu.make_async_copy(upd_h, upd, load_sem.at[8])
+    rows_in.start()
     for load in loads:
         load.start()
 
@@ -319,6 +340,7 @@
 
         lax.fori_loop(lo, hi, one, 0)
 
+    rows_in.wait()
     gather(0, upd)
     recv[0] = send[0]
     pl.semaphore_wait(barrier, 13)
@@ -343,6 +365,7 @@
     lax.fori_loop(0, ROWS // CROWS, spread_own, 0)
 
     rest = pltpu.make_async_copy(recv, table, out_sem.at[0])
+    nat_out = pltpu.make_async_copy(nat, natural, out_sem.at[1])
 
     def step(s, _):
         j = s - 1
@@ -364,33 +387,51 @@
         def _():
             rest.start()
 
-        b = (2 * s + 1) // 5
+        b = (2 * s + 1) // 5 + s // 14 - s // 15
 
         @pl.when(step_of(b) == s)
         def _():
             at = pl.ds(pl.multiple_of(b * BLOCK, BLOCK), BLOCK)
             dec[at] = decode_block(b, order_s, tab, picked, sides, wall, hidden, head)
-            pltpu.make_async_copy(dec.at[at], decoded.at[at], out_sem.at[1]).start()
+
+        @pl.when(s == step_of(EARLY - 1) + 1)
+        def _():
+            def back(n, _):
+                for u in range(64):
+                    j = n * 64 + u
+                    nat[pl.ds(j, 1), :] = dec[pl.ds(place_s[j], 1), :]
+                return 0
+
+            lax.fori_loop(0, OBS // 64, back, 0)
+            nat_out.start()
 
         return 0
 
     lax.fori_loop(0, EVENTS + 1, step, 0)
+    last = pltpu.make_async_copy(dec.at[pl.ds(EARLY * BLOCK, LATE)], late, out_sem.at[2])
+    last.start()
     rest.wait()
-    pltpu.make_async_copy(dec, decoded, out_sem.at[1]).wait()
+    nat_out.wait()
+    last.wait()
     pltpu.make_async_copy(send.at[pl.ds(0, NDEV - 1)], send.at[pl.ds(0, NDEV - 1)], send_sem).wait()
 
 
-def exchange(upd, send_rows, order, feat, embed, w_dec, w_feat, w_head):
+def exchange(upd, send_rows, order, place, feat, embed, w_dec, w_feat, w_head):
     vmem, any_ = pl.BlockSpec(memory_space=pltpu.VMEM), pl.BlockSpec(memory_space=pl.ANY)
     return pl.pallas_call(
         exchange_kernel,
         out_shape=(
             jax.ShapeDtypeStruct((NDEV, CAP, D), BF16),
             jax.ShapeDtypeStruct((OBS, 128), F32),
+            jax.ShapeDtypeStruct((LATE, 128), F32),
         ),
-        in_specs=[vmem, vmem, pl.BlockSpec(memory_space=pltpu.SMEM), vmem] + [any_] * 5,
-        out_specs=(any_, any_),
+        in_specs=[any_, vmem] + [any_] * 8,
+        out_specs=(any_, any_, any_),
         scratch_shapes=[
+            pltpu.VMEM((ROWS, D), BF16),
+            pltpu.SMEM((96 * 128,), jnp.int32),
+            pltpu.VMEM((96, 128), jnp.int32),
+            pltpu.SMEM((48 * 128,), jnp.int32),
             pltpu.VMEM((NDEV, CAP, D), BF16),
             pltpu.VMEM((NDEV, CAP, D), BF16),
             pltpu.VMEM((4 * TABLE + 8, 128), F32),
@@ -404,119 +445,115 @@
             pltpu.VMEM((FF, 128), BF16),
             pltpu.VMEM((32, FF), F32),
             pltpu.VMEM((OBS, 128), F32),
-            pltpu.SemaphoreType.DMA((5,)),
+            pltpu.VMEM((OBS, 128), F32),
+            pltpu.SemaphoreType.DMA((9,)),
             pltpu.SemaphoreType.DMA,
             pltpu.SemaphoreType.DMA((CHUNKS,)),
-            pltpu.SemaphoreType.DMA((2,)),
+            pltpu.SemaphoreType.DMA((3,)),
             pltpu.SemaphoreType.REGULAR,
             pltpu.SemaphoreType.REGULAR,
         ],
         compiler_params=pltpu.CompilerParams(collective_id=1, has_side_effects=True, vmem_limit_bytes=60 << 20),
         name="exchange",
-    )(upd, send_rows.T, order.reshape(-1), order, feat, embed, w_dec, w_feat, w_head)
+    )(upd, send_rows.T, order.reshape(-1), order, place.reshape(-1), feat, embed, w_dec, w_feat, w_head)
 
 
 def finish_kernel(
-    place, order, upd, dec_in, table, feat, embed, w_dec, w_feat, w_head, latent_out, decoded,
-    dec, lat, tabb, tab, featb, feats, sfeats, picked, sides, wall, hidden, head, emb, order_s, order_v, sem, load_sem,
+    place, order, order_h, upd, natural, late, table, feat, embed, w_dec, w_feat, w_head, latent_out, decoded,
+    buf, tail, lat, tabb, tab, featb, feats, sfeats, picked, sides, wall, hidden, head, emb, order_s, order_v, sem, load_sem,
 ):
-    i = pl.program_id(0)
-    keep = pltpu.make_async_copy(lat, latent_out, sem.at[2])
-
-    @pl.when(i == 0)
+    ins = [
+        pltpu.make_async_copy(natural, buf, sem.at[1]),
+        pltpu.make_async_copy(late, tail, sem.at[2]),
+        pltpu.make_async_copy(upd, lat, sem.at[0]),
+    ]
+    for copy in ins:
+        copy.start()
+    for copy in ins:
+        copy.wait()
+    keep = pltpu.make_async_copy(lat, latent_out, sem.at[3])
+    keep.start()
+
+    def scatter(numbers, start, n):
+        def move(i, _):
+            for u in range(64):
+                j = i * 64 + u
+                buf[pl.ds(numbers[start + j], 1), :] = tail[pl.ds(j, 1), :]
+            return 0
+
+        lax.fori_loop(0, n // 64, move, 0)
+
+    scatter(place, 40 * 128, LATE)
+
+    def missed(b):
+        last = place[(32 + b) * 128 + 127]
+        return jnp.where(last < ROWS, 0, 1 + (last - ROWS) // CROWS) > step_of(b)
+
+    any_missed = missed(0)
+    for b in range(1, BLOCKS):
+        any_missed = jnp.logical_or(any_missed, missed(b))
+
+    @pl.when(any_missed)
     def _():
-        first = pltpu.make_async_copy(upd, lat, sem.at[0])
-        second = pltpu.make_async_copy(dec_in, dec, sem.at[1])
-        second.start()
-        first.start()
-        first.wait()
-        keep.start()
-        second.wait()
-
-        def missed(b):
-            last = place[(32 + b) * 128 + 127]
-            return jnp.where(last < ROWS, 0, 1 + (last - ROWS) // CROWS) > step_of(b)
-
-        any_missed = missed(0)
-        for b in range(1, BLOCKS):
-            any_missed = jnp.logical_or(any_missed, missed(b))
-
-        @pl.when(any_missed)
-        def _():
-            loads = [
-                pltpu.make_async_copy(feat, featb, load_sem.at[0]),
-                pltpu.make_async_copy(embed, emb, load_sem.at[1]),
-                pltpu.make_async_copy(w_dec, wall.at[pl.ds(0, 512)], load_sem.at[2]),
-                pltpu.make_async_copy(w_feat, wall.at[pl.ds(512, 128)], load_sem.at[3]),
-                pltpu.make_async_copy(w_head, head, load_sem.at[4]),
-                pltpu.make_async_copy(table, tabb, load_sem.at[5]),
-                pltpu.make_async_copy(order, order_v, load_sem.at[6]),
-            ]
-            for load in loads:
-                load.start()
-            for load in loads:
-                load.wait()
-            load_decoder(emb, wall)
-            feats[...] = featb[...].astype(F32)
-
-            def to_scalar(n, _):
-                to = order_s.at[pl.ds(pl.multiple_of(n * 128, 128), 128)]
-                copy = pltpu.make_async_copy(order_v.at[n], to, load_sem.at[7])
-                copy.start()
-                copy.wait()
-                return 0
-
-            lax.fori_loop(0, 64, to_scalar, 0)
-            pick_sides(order_s, order_v, feats, sfeats, sides)
-
-            def spread_own(n, _):
-                widen(tab, n * CROWS, lat[pl.ds(pl.multiple_of(n * CROWS, CROWS), CROWS)])
-                return 0
-
-            lax.fori_loop(0, ROWS // CROWS, spread_own, 0)
-
-            def spread(n, _):
-                widen(tab, ROWS + n * CROWS, tabb[pl.ds(n * PER, PER)].reshape(CROWS, D))
-                return 0
-
-            lax.fori_loop(0, CHUNKS, spread, 0)
-
-            def again(b, _):
-                @pl.when(missed(b))
-                def _():
-                    dec[pl.ds(pl.multiple_of(b * BLOCK, BLOCK), BLOCK)] = decode_block(
-                        b, order_s, tab, picked, sides, wall, hidden, head
-                    )
-
-                return 0
-
-            lax.fori_loop(0, BLOCKS, again, 0)
-
-    def back(n, _):
-        for u in range(32):
-            j = n * 32 + u
-            decoded[pl.ds(j, 1), :] = dec[pl.ds(place[i * OUT + j], 1), :]
-        return 0
-
-    lax.fori_loop(0, OUT // 32, back, 0)
-
-    @pl.when(i == OBS // OUT - 1)
-    def _():
-        keep.wait()
-
-
-def finish(place, order, upd, dec, table, feat, embed, w_dec, w_feat, w_head):
+        loads = [
+            pltpu.make_async_copy(feat, featb, load_sem.at[0]),
+            pltpu.make_async_copy(embed, emb, load_sem.at[1]),
+            pltpu.make_async_copy(w_dec, wall.at[pl.ds(0, 512)], load_sem.at[2]),
+            pltpu.make_async_copy(w_feat, wall.at[pl.ds(512, 128)], load_sem.at[3]),
+            pltpu.make_async_copy(w_head, head, load_sem.at[4]),
+            pltpu.make_async_copy(table, tabb, load_sem.at[5]),
+            pltpu.make_async_copy(order, order_v, load_sem.at[6]),
+            pltpu.make_async_copy(order_h, order_s, load_sem.at[7]),
+        ]
+        for load in loads:
+            load.start()
+        for load in loads:
+            load.wait()
+        load_decoder(emb, wall)
+        feats[...] = featb[...].astype(F32)
+        pick_sides(order_s, order_v, feats, sfeats, sides)
+
+        def spread_own(n, _):
+            widen(tab, n * CROWS, lat[pl.ds(pl.multiple_of(n * CROWS, CROWS), CROWS)])
+            return 0
+
+        lax.fori_loop(0, ROWS // CROWS, spread_own, 0)
+
+        def spread(n, _):
+            widen(tab, ROWS + n * CROWS, tabb[pl.ds(n * PER, PER)].reshape(CROWS, D))
+            return 0
+
+        lax.fori_loop(0, CHUNKS, spread, 0)
+
+        def again(b, _):
+            @pl.when(missed(b))
+            def _():
+                tail[0:BLOCK] = decode_block(b, order_s, tab, picked, sides, wall, hidden, head)
+                scatter(order_s, OBS + b * BLOCK, BLOCK)
+
+            return 0
+
+        lax.fori_loop(0, BLOCKS, again, 0)
+
+    done = pltpu.make_async_copy(buf, decoded, sem.at[4])
+    done.start()
+    done.wait()
+    keep.wait()
+
+
+def finish(place, order, upd, natural, late, table, feat, embed, w_dec, w_feat, w_head):
     any_ = pl.BlockSpec(memory_space=pl.ANY)
     return pl.pallas_call(
         finish_kernel,
         out_shape=(jax.ShapeDtypeStruct((ROWS, D), BF16), jax.ShapeDtypeStruct((OBS, 128), F32)),
         grid_spec=pltpu.PrefetchScalarGridSpec(
             num_scalar_prefetch=1,
-            grid=(OBS // OUT,),
-            in_specs=[any_] * 9,
-            out_specs=(any_, pl.BlockSpec((OUT, 128), lambda i, _: (i, 0))),
+            grid=(1,),
+            in_specs=[any_] * 11,
+            out_specs=(any_, any_),
             scratch_shapes=[
                 pltpu.VMEM((OBS, 128), F32),
+                pltpu.VMEM((LATE, 128), F32),
                 pltpu.VMEM((ROWS, D), BF16),
                 pltpu.VMEM((NDEV, CAP, D), BF16),
                 pltpu.VMEM((4 * TABLE + 8, 128), F32),
@@ -529,21 +566,21 @@
                 pltpu.VMEM((BLOCK, FF), BF16),
                 pltpu.VMEM((FF, 128), BF16),
                 pltpu.VMEM((32, FF), F32),
-                pltpu.SMEM((2 * OBS,), jnp.int32),
+                pltpu.SMEM((96 * 128,), jnp.int32),
                 pltpu.VMEM((96, 128), jnp.int32),
-                pltpu.SemaphoreType.DMA((3,)),
+                pltpu.SemaphoreType.DMA((5,)),
                 pltpu.SemaphoreType.DMA((8,)),
             ],
         ),
         compiler_params=pltpu.CompilerParams(vmem_limit_bytes=56 << 20, dimension_semantics=("arbitrary",)),
         name="finish",
-    )(place.reshape(-1), order, upd, dec, table, feat, embed, w_dec, w_feat, w_head)
+    )(place.reshape(-1), order, order.reshape(-1), upd, natural, late, table, feat, embed, w_dec, w_feat, w_head)
 
 
 def local(latent, norm_gain, w_in, w_out, send_rows, obs_src, obs_feat, obs_inst, inst_embed, w_dec, w_feat, w_head):
     upd, order, place = process(latent, norm_gain, w_in, w_out, obs_src, obs_inst)
-    table, dec = exchange(upd, send_rows, order, obs_feat, inst_embed, w_dec, w_feat, w_head)
-    return finish(place, order, upd, dec, table, obs_feat, inst_embed, w_dec, w_feat, w_head)
+    table, natural, late = exchange(upd, send_rows, order, place, obs_feat, inst_embed, w_dec, w_feat, w_head)
+    return finish(place, order, upd, natural, late, table, obs_feat, inst_embed, w_dec, w_feat, w_head)
 
 
 def solution(mesh):

time: 105 us -> 104 us (level)
  the two profiles are of different devices: /device:TPU:1 before, /device:TPU:36 now
where the time goes in v4:
time: 104 us
  Pallas kernels  103 us (99%)
    pallas_call x1, Pallas kernels, exchange(): pl.pallas_call(exchange_kernel, out_shape=(jax.ShapeDtypeStruct((NDEV, CA...  70.9 us
    pallas_call x1, Pallas kernels, process(): pl.pallas_call(process_kernel, out_shape=(jax.ShapeDtypeStruct((ROWS, D),...  26.4 us
    pallas_call x1, Pallas kernels, finish(): pl.pallas_call(finish_kernel, out_shape=(jax.ShapeDtypeStruct((ROWS, D),...  5.6 us

profile of v4, /device:TPU:36, one launch (start us, length us, event | category | flops | bytes accessed | tf_op | source)
XLA Modules:
  0.0 103.6 jit_solution(7505956898613728689)
XLA Ops:
  0.6 26.4 %process.1 = (bf16[1024,512]{1,0:T(8,128)(2,1)}, s32[96,128]{1,0:T(8,128)}, s32[48,128]{1,0:T(8,128)}) custom-call(bf16[1024,512]{1,0:T(8,128)(2,1)} %latent_h.1, f32[1,512]{1,0:T(1,128)} %bitcast.17, bf16[16,32,512]{2,1,0:T(8,128)(2,1)} %bitcast.10, bf16[16,32,512]{2,1,0:T(8,128)(2,1)} %bitcast.11, s32[32,128]{1,0:T(8,128)} %bitcast.14, s32[32,128]{1,0:T(8,128)} %bitcast.15), custom_call_target="tpu_custom_call" | custom-call | tf_op jit(solution)/shard_map/process/pallas_call | solution.py:256
  27.0 70.9 %exchange.1 = (bf16[128,32,512]{2,1,0:T(8,128)(2,1)}, f32[4096,128]{1,0:T(8,128)}, f32[1024,128]{1,0:T(8,128)}) custom-call(bf16[1024,512]{1,0:T(8,128)(2,1)} %get-tuple-element.10.upd_h.upd, s32[32,128]{1,0:T(8,128)} %bitcast.16, s32[12288]{0:T(1024)} %bitcast.8, s32[96,128]{1,0:T(8,128)} %get-tuple-element.9.order_vh.order, s32[6144]{0:T(1024)} %bitcast.12, ...), custom_call_target="tpu_custom_call" | custom-call | tf_op jit(solution)/shard_map/exchange/pallas_call | solution.py:421
  97.9 5.6 %finish.1 = (bf16[1024,512]{1,0:T(8,128)(2,1)}, f32[4096,128]{1,0:T(8,128)}) custom-call(s32[6144]{0:T(1024)} %bitcast.13, s32[96,128]{1,0:T(8,128)} %get-tuple-element.9.order_vh.order, s32[12288]{0:T(1024)} %bitcast.9, bf16[1024,512]{1,0:T(8,128)(2,1)} %get-tuple-element.10.upd_h.upd, f32[4096,128]{1,0:T(8,128)} %get-tuple-element.11.natural, ...), custom_call_target="tpu_custom_call" | custom-call | tf_op jit(solution)/shard_map/finish/pallas_call | solution.py:546

commit v5 on v4

--- a/solution.py
+++ b/solution.py
@@ -16,7 +16,7 @@
 PER = 8
 CHUNKS = NDEV // PER
 CROWS = PER * CAP
-MUL, INV = 37, 45
+MUL, INV = 11, 35
 TABLE = ROWS + NDEV * CAP
 OBS = 4096
 BLOCK = 512

time: 104 us -> 101 us (0.971)
  the two profiles are of different devices: /device:TPU:36 before, /device:TPU:27 now
where the time goes in v5:
time: 101 us; the launch traced here: 100 us
  Pallas kernels  99.3 us (98%)
    pallas_call x1, Pallas kernels, exchange(): pl.pallas_call(exchange_kernel, out_shape=(jax.ShapeDtypeStruct((NDEV, CA...  66.5 us
    pallas_call x1, Pallas kernels, process(): pl.pallas_call(process_kernel, out_shape=(jax.ShapeDtypeStruct((ROWS, D),...  27.2 us
    pallas_call x1, Pallas kernels, finish(): pl.pallas_call(finish_kernel, out_shape=(jax.ShapeDtypeStruct((ROWS, D),...  5.6 us

profile of v5, /device:TPU:27, one launch (start us, length us, event | category | flops | bytes accessed | tf_op | source)
XLA Modules:
  0.0 100.1 jit_solution(15571883426642024128)
XLA Ops:
  0.6 27.2 %process.1 = (bf16[1024,512]{1,0:T(8,128)(2,1)}, s32[96,128]{1,0:T(8,128)}, s32[48,128]{1,0:T(8,128)}) custom-call(bf16[1024,512]{1,0:T(8,128)(2,1)} %latent_h.1, f32[1,512]{1,0:T(1,128)} %bitcast.17, bf16[16,32,512]{2,1,0:T(8,128)(2,1)} %bitcast.10, bf16[16,32,512]{2,1,0:T(8,128)(2,1)} %bitcast.11, s32[32,128]{1,0:T(8,128)} %bitcast.14, s32[32,128]{1,0:T(8,128)} %bitcast.15), custom_call_target="tpu_custom_call" | custom-call | tf_op jit(solution)/shard_map/process/pallas_call | solution.py:256
  27.8 66.5 %exchange.1 = (bf16[128,32,512]{2,1,0:T(8,128)(2,1)}, f32[4096,128]{1,0:T(8,128)}, f32[1024,128]{1,0:T(8,128)}) custom-call(bf16[1024,512]{1,0:T(8,128)(2,1)} %get-tuple-element.10.upd_h.upd, s32[32,128]{1,0:T(8,128)} %bitcast.16, s32[12288]{0:T(1024)} %bitcast.8, s32[96,128]{1,0:T(8,128)} %get-tuple-element.9.order_vh.order, s32[6144]{0:T(1024)} %bitcast.12, ...), custom_call_target="tpu_custom_call" | custom-call | tf_op jit(solution)/shard_map/exchange/pallas_call | solution.py:421
  94.3 5.6 %finish.1 = (bf16[1024,512]{1,0:T(8,128)(2,1)}, f32[4096,128]{1,0:T(8,128)}) custom-call(s32[6144]{0:T(1024)} %bitcast.13, s32[96,128]{1,0:T(8,128)} %get-tuple-element.9.order_vh.order, s32[12288]{0:T(1024)} %bitcast.9, bf16[1024,512]{1,0:T(8,128)(2,1)} %get-tuple-element.10.upd_h.upd, f32[4096,128]{1,0:T(8,128)} %get-tuple-element.11.natural, ...), custom_call_target="tpu_custom_call" | custom-call | tf_op jit(solution)/shard_map/finish/pallas_call | solution.py:546
